TPU v7x, 256 devices: a whole 4x4x8 slice. The times are simulated.
256 devices in a mesh: seq: 64 (over z, x_hi, y), head: 4 (over x_lo, core).
Axes of the slice: x: 4 (x_hi: 2, x_lo: 2; x = x_hi * 2 + x_lo), y: 4, z: 8, core: 2. Of those that a mesh axis runs over, the one named last changes fastest.
Arguments:
- queries: bfloat16 [1, 32768, 1024], P(None, 'seq', 'head'), may hold values from -40 to 40
- key_vectors: bfloat16 [1, 32768, 1024], P(None, 'seq', 'head'), may hold values from -40 to 40
- value_vectors: bfloat16 [1, 32768, 1024], P(None, 'seq', 'head'), may hold values from -6 to 6
- out_weight: bfloat16 [1024, 1024], replicated, may hold values from -0.1875 to 0.1875
Outputs:
- layer_output: bfloat16 [1, 32768, 1024], P(None, ('seq', 'head'))
All inputs are finite; a program needn't handle non-finite values.
Results may differ from a plain program's by a relative error of at most 0.038.
Values may be sent and summed in bfloat16 or wider, within the bound.
A program may use at most 192 MiB of HBM per device.

v0:
```python
import jax
import jax.numpy as jnp
from jax import lax
from jax.sharding import PartitionSpec as P

HD = 64
BLOCK = 128
LEVELS = 4


neg_fill = -1e30
root_half = 0.7071067811865476


def swapped(block, axis, bit):
    count = lax.axis_size(axis)
    route = []
    for low in range(count):
        high = low | 1 << bit
        if high != low and high < count:
            route += [(low, high), (high, low)]
    return lax.ppermute(block, axis, route)


def extended(cells, sides, width):
    for axis, dim in sides:
        count = lax.axis_size(axis)
        ends = count - 1
        head = lax.slice_in_dim(cells, 0, width, axis=dim)
        tail = lax.slice_in_dim(cells, cells.shape[dim] - width, cells.shape[dim], axis=dim)
        cells = jnp.concatenate(
            [
                lax.ppermute(tail, axis, [(i, (i + 1) % count) for i in range(ends)]),
                cells,
                lax.ppermute(head, axis, [((i + 1) % count, i) for i in range(ends)]),
            ],
            axis=dim,
        )
    return cells


def pooled(field):
    shape = field.shape
    pairs = field.astype(jnp.float32).reshape(shape[:-2] + (shape[-2] // 2, 2, shape[-1]))
    return ((pairs[..., 0, :] + pairs[..., 1, :]) * root_half).astype(jnp.bfloat16)


def heads_first(field):
    samples, shard_rows, features = field.shape
    return jnp.transpose(field.reshape(samples, shard_rows, features // HD, HD), (0, 2, 1, 3))


def attend(query_blocks, key_blocks, value_blocks):
    samples, heads_here, blocks, query_count, depth = query_blocks.shape
    scaling = HD ** (-0.5)
    scores = (
        jnp.einsum(
            "shnqd,shnkd->shnqk", query_blocks, key_blocks, preferred_element_type=jnp.float32
        )
        * scaling
    )
    row_max = jnp.max(scores, axis=-1)
    chances = jnp.exp(scores - row_max[..., None]).astype(jnp.bfloat16)
    row_sum = jnp.sum(chances, axis=-1, dtype=jnp.float32)
    numerator = jnp.einsum(
        "shnqk,shnkd->shnqd", chances, value_blocks, preferred_element_type=jnp.float32
    )
    return (
        row_max.reshape(samples, heads_here, blocks * query_count),
        numerator.reshape(samples, heads_here, blocks * query_count, depth),
        row_sum.reshape(samples, heads_here, blocks * query_count),
    )


def combined(terms):
    expanded = [jnp.repeat(record[1], 2 ** record[0], axis=2) for record in terms]
    top_max = expanded[0]
    for other_max in expanded[1:]:
        top_max = jnp.maximum(top_max, other_max)
    numerator = jnp.zeros(terms[0][2].shape, jnp.float32)
    denominator = jnp.zeros(top_max.shape, jnp.float32)
    for record, fine_max in zip(terms, expanded):
        factor = jnp.exp(fine_max - top_max)
        numerator = numerator + jnp.repeat(record[2], 2 ** record[0], axis=2) * factor[..., None]
        denominator = denominator + jnp.repeat(record[3], 2 ** record[0], axis=2) * factor
    return (numerator / denominator[..., None]).astype(jnp.bfloat16)


def fetch_sibling(piece, spread, position):
    top_bit = spread.bit_length() - 1
    current = swapped(piece, "seq", top_bit)
    for low_bit in range(top_bit):
        partner_piece = swapped(current, "seq", low_bit)
        high_half = position // 2**low_bit % 2
        current = jnp.where(
            high_half == 0,
            jnp.concatenate([current, partner_piece], axis=3),
            jnp.concatenate([partner_piece, current], axis=3),
        )
    return current[:, :, :, None]


def per_device(queries, key_vectors, value_vectors, out_weight):
    samples, shard_rows, features = queries.shape
    block_rows = BLOCK
    position = lax.axis_index("seq")
    devices_seq = lax.axis_size("seq")
    blocks = shard_rows // block_rows
    heads_here = features // HD
    scaling = HD ** (-0.5)
    query_heads = heads_first(queries)
    level_kv = jnp.stack([heads_first(key_vectors), heads_first(value_vectors)])
    padded = extended(level_kv, (("seq", 3),), block_rows)

    def view(offset):
        return padded[:, :, :, offset : offset + shard_rows].reshape(
            2, samples, heads_here, blocks, block_rows, HD
        )

    sides = [view(0), view(block_rows), view(2 * block_rows)]
    query_blocks = query_heads.reshape(samples, heads_here, blocks, block_rows, HD)
    scores = (
        jnp.concatenate(
            [
                jnp.einsum(
                    "shnqd,shnkd->shnqk", query_blocks, side[0], preferred_element_type=jnp.float32
                )
                for side in sides
            ],
            axis=-1,
        )
        * scaling
    )
    global_ids = position * blocks + jnp.arange(blocks)
    left_ok = jnp.broadcast_to((global_ids > 0)[:, None], (blocks, block_rows))
    right_ok = jnp.broadcast_to(
        (global_ids < devices_seq * blocks - 1)[:, None], (blocks, block_rows)
    )
    allowed = jnp.concatenate(
        [left_ok, jnp.ones((blocks, block_rows), jnp.bool_), right_ok], axis=1
    )
    scores = jnp.where(allowed[None, None, :, None, :], scores, neg_fill)
    near_max = jnp.max(scores, axis=-1)
    chances = jnp.exp(scores - near_max[..., None]).astype(jnp.bfloat16)
    near_sum = jnp.sum(chances, axis=-1, dtype=jnp.float32)
    near_numer = jnp.zeros((samples, heads_here, blocks, block_rows, HD), jnp.float32)
    for index, side in enumerate(sides):
        near_numer = near_numer + jnp.einsum(
            "shnqk,shnkd->shnqd",
            chances[..., index * block_rows : (index + 1) * block_rows],
            side[1],
            preferred_element_type=jnp.float32,
        )
    terms = [
        (
            0,
            near_max.reshape(samples, heads_here, shard_rows),
            near_numer.reshape(samples, heads_here, shard_rows, HD),
            near_sum.reshape(samples, heads_here, shard_rows),
        )
    ]
    level_q = query_heads
    pooled_rows = shard_rows
    for ladder in range(1, LEVELS + 1):
        level_q = pooled(level_q)
        pooled_rows = shard_rows >> ladder
        if pooled_rows >= 2 * block_rows:
            level_kv = pooled(level_kv)
            grouped = level_kv.reshape(
                2, samples, heads_here, pooled_rows // (2 * block_rows), 2, block_rows, HD
            )
            partner = grouped[:, :, :, :, ::-1].reshape(
                2, samples, heads_here, pooled_rows // block_rows, block_rows, HD
            )
            level_blocks = level_q.reshape(
                samples, heads_here, pooled_rows // block_rows, block_rows, HD
            )
        else:
            level_blocks = level_q.reshape(samples, heads_here, 1, pooled_rows, HD)
            level_kv = pooled(level_kv)
            partner = fetch_sibling(level_kv, block_rows // pooled_rows, position)
        terms.append((ladder,) + attend(level_blocks, partner[0], partner[1]))
    summit = lax.all_gather(level_kv, "seq", axis=3, tiled=True)
    top_queries = level_q.reshape(samples, heads_here, 1, pooled_rows, HD)
    terms.append((LEVELS,) + attend(top_queries, summit[0][:, :, None], summit[1][:, :, None]))
    attended = jnp.transpose(combined(terms), (0, 2, 1, 3)).reshape(samples, shard_rows, features)
    return jnp.einsum(
        "brf,fg->brg",
        lax.all_to_all(attended, "head", split_axis=1, concat_axis=2, tiled=True),
        out_weight,
        preferred_element_type=jnp.float32,
    ).astype(jnp.bfloat16)


def solution(mesh):
    return jax.shard_map(
        per_device,
        mesh=mesh,
        in_specs=(P(None, "seq", "head"), P(None, "seq", "head"), P(None, "seq", "head"), P()),
        out_specs=P(None, ("seq", "head"), None),
        check_vma=False,
    )
```

profile of v0, /device:TPU:1, one launch (start us, length us, event | category | flops | bytes accessed | tf_op | source)
XLA Modules:
  0.0 199.0 jit_solution(9807319620057885751)
XLA Ops:
  10.2 2.6 %maximum_convert_fusion = f32[2,1,4,256,2,64]{5,4,3,2,1,0:T(2,128)S(1)} fusion(bf16[1,1,4,256,2,64]{5,4,3,2,1,0:T(2,128)(2,1)S(1)} %bitcast.216, bf16[1,1,4,256,2,64]{5,4,3,2,1,0:T(2,128)(2,1)} %bitcast.217), kind=kLoop, calls=%fused_computation.19 | loop fusion | flops 524288 | bytes 1572864 | tf_op jit(solution)/shard_map/convert_element_type | solution.py:44
  12.8 2.7 %fusion.52 = (f32[2,1,4,256,1,64]{5,4,3,2,1,0:T(1,128)S(1)}, bf16[2,1,4,256,1,64]{5,4,3,2,1,0:T(2,128)(2,1)}) fusion(f32[2,1,4,256,2,64]{5,4,3,2,1,0:T(2,128)S(1)} %maximum_convert_fusion), kind=kLoop, calls=%fused_computation.116 | loop fusion | flops 524288 | bytes 1835008 | tf_op jit(solution)/shard_map/convert_element_type | solution.py:44
  15.5 1.8 fusion.57
  29.2 3.7 %collective-permute-start.5 = (bf16[2,1,4,32,64]{3,4,2,1,0:T(8,128)(2,1)}, bf16[2,1,4,32,64]{3,4,2,1,0:T(8,128)(2,1)}, u32[]{:S(2)}, u32[]{:S(2)}) collective-permute-start(bf16[2,1,4,32,64]{3,4,2,1,0:T(8,128)(2,1)} %bitcast.36), channel_id=1, source_target_pairs={{0,16},{16,0},{4,20},{20,4},{8,24},{24,8},{12,28},{28,12},{32,48},... | collective-permute-start | bytes 98312 | tf_op jit(solution)/shard_map/ppermute | solution.py:22
  32.9 2.9 %collective-permute-start.3 = (bf16[2,1,4,64,64]{3,4,2,1,0:T(8,128)(2,1)}, bf16[2,1,4,64,64]{3,4,2,1,0:T(8,128)(2,1)}, u32[]{:S(2)}, u32[]{:S(2)}) collective-permute-start(bf16[2,1,4,64,64]{3,4,2,1,0:T(8,128)(2,1)} %bitcast.32), channel_id=1, source_target_pairs={{0,8},{8,0},{4,12},{12,4},{16,24},{24,16},{20,28},{28,20},{32,40},... | collective-permute-start | bytes 196616 | tf_op jit(solution)/shard_map/ppermute | solution.py:22
  38.2 4.6 %collective-permute-start = (bf16[2,1,4,128,64]{3,4,2,1,0:T(8,128)(2,1)}, bf16[2,1,4,128,64]{3,4,2,1,0:T(8,128)(2,1)}, u32[]{:S(2)}, u32[]{:S(2)}) collective-permute-start(bf16[2,1,4,128,64]{3,4,2,1,0:T(8,128)(2,1)} %get-tuple-element.32), channel_id=1, source_target_pairs={{0,4},{4,8},{8,12},{12,16},{16,20},{20,24},{24,28},{28,32},{32,36}... | collective-permute-start | bytes 393224 | tf_op jit(solution)/shard_map/ppermute | solution.py:33
  44.2 3.3 %fusion.56 = (f32[1,4,256,1,64]{4,3,2,1,0:T(1,128)S(1)}, f32[1,4,256,1,64]{4,3,2,1,0:T(1,128)}) fusion(f32[1,4,256,2,64]{4,3,2,1,0:T(2,128)} %bitcast.204), kind=kLoop, calls=%fused_computation.119 | loop fusion | bytes 1048576 | tf_op jit(solution)/shard_map/slice | solution.py:45
  47.5 1.9 copy.357
  54.6 2.6 %fusion.58 = (f32[1,4,128,1,64]{4,3,2,1,0:T(1,128)}, f32[1,4,128,1,64]{4,3,2,1,0:T(1,128)}) fusion(f32[1,4,128,2,64]{4,3,2,1,0:T(2,128)} %bitcast.212), kind=kLoop, calls=%fused_computation.121 | loop fusion | bytes 524288 | tf_op jit(solution)/shard_map/slice | solution.py:45
  57.2 1.7 copy.359
  58.9 1.7 copy.360
  62.4 2.0 fusion.50
  65.1 2.0 %fusion.55 = (bf16[1,1,4,256,1,64]{5,4,3,2,1,0:T(2,128)(2,1)}, bf16[1,1,4,256,1,64]{5,4,3,2,1,0:T(2,128)(2,1)}) fusion(bf16[2,1,4,256,1,64]{5,4,3,2,1,0:T(2,128)(2,1)S(1)} %copy-done.2), kind=kLoop, calls=%fused_computation.118 | loop fusion | bytes 524288 | tf_op jit(solution)/shard_map/slice | solution.py:182
  77.2 2.4 %broadcast_in_dim.134 = f32[4,256,2,64]{3,2,1,0:T(2,128)} broadcast(f32[4,256,64]{2,1,0:T(8,128)} %bitcast.211), dimensions={0,1,3} | broadcast | bytes 786432 | tf_op jit(solution)/shard_map/broadcast_in_dim | solution.py:84
  79.5 2.4 %copy.332 = f32[1,4,512,64]{2,3,1,0:T(8,128)} copy(f32[1,4,512,64]{3,2,1,0:T(8,128)} %bitcast.205) | data formatting | bytes 1048576 | tf_op jit(solution)/shard_map/broadcast_in_dim | solution.py:84
  82.7 1.7 broadcast_in_dim.144
  89.8 4.2 %collective-permute-start.7 = (bf16[2,1,4,64,64]{3,4,2,1,0:T(8,128)(2,1)S(1)}, bf16[2,1,4,64,64]{3,4,2,1,0:T(8,128)(2,1)S(1)}, u32[]{:S(2)}, u32[]{:S(2)}) collective-permute-start(bf16[2,1,4,64,64]{3,4,2,1,0:T(8,128)(2,1)S(1)} %maximum_select_fusion.2), channel_id=1, source_target_pairs={{0,8},{8,0},{4,12},{12,4},{16,24},{24,16},{20,28},{28,20},{32,40},... | collective-permute-start | bytes 196616 | tf_op jit(solution)/shard_map/ppermute | solution.py:22
  99.4 2.4 %copy.337 = f32[1,4,512,64]{2,3,1,0:T(8,128)} copy(f32[1,4,512,64]{3,2,1,0:T(8,128)} %bitcast.206) | data formatting | bytes 1048576 | tf_op jit(solution)/shard_map/broadcast_in_dim | solution.py:84
  105.4 2.4 %copy.336 = f32[1,4,512,64]{2,3,1,0:T(8,128)} copy(f32[1,4,512,64]{3,2,1,0:T(8,128)} %broadcast_bitcast_fusion) | data formatting | bytes 1048576 | tf_op jit(solution)/shard_map/broadcast_in_dim | solution.py:84
  111.8 2.4 %copy.335 = f32[1,4,512,64]{2,3,1,0:T(8,128)} copy(f32[1,4,512,64]{3,2,1,0:T(8,128)} %bitcast.203) | data formatting | bytes 1048576 | tf_op jit(solution)/shard_map/broadcast_in_dim | solution.py:84
  114.2 2.1 %pad_maximum_fusion = (bf16[1,1,4,512,64]{3,4,2,1,0:T(8,128)(2,1)}, bf16[1,1,4,512,64]{3,4,2,1,0:T(8,128)(2,1)}, bf16[1,1,4,512,64]{3,4,2,1,0:T(8,128)(2,1)}, bf16[1,1,4,512,64]{3,4,2,1,0:T(8,128)(2,1)}) fusion(bf16[2,1,4,128,64]{3,4,2,1,0:T(8,128)(2,1)} %collective-permute-done.1, bf16[1,1,4,512,64]{3,4,2,1,0:T(8,128)(2,1)S(1)} %bitcast.198, ...), kind=kLoop, calls=%fused_computation.34 | loop fusion | flops 3145728 | bytes 1835008 | tf_op jit(solution)/shard_map/concatenate | solution.py:31
  116.3 1.8 reshape.1719
  118.0 1.7 reshape.1715
  119.8 1.8 reshape.1721
  121.6 1.7 reshape.1725
  133.4 24.3 %all-gather.3.cloned.1.call-done = bf16[2,1,4,2048,1,64]{5,2,4,1,0,3:T(4,128)(2,1)} async-done(((bf16[2,1,4,32,1,64]{5,2,4,1,0,3:T(4,128)(2,1)}), bf16[2,1,4,2048,1,64]{5,2,4,1,0,3:T(4,128)(2,1)}) %all-gather.3.cloned.1.call-update) | async-done | bytes 2097168 | tf_op jit(solution)/shard_map/all_gather | solution.py:183
  157.7 4.4 %fusion.54 = (bf16[1,1,4,2048,1,64]{5,2,4,1,0,3:T(4,128)(2,1)}, bf16[1,1,4,2048,1,64]{5,2,4,1,0,3:T(4,128)(2,1)}) fusion(bf16[2,1,4,2048,1,64]{5,2,4,1,0,3:T(4,128)(2,1)} %all-gather.3.cloned.1.call-done), kind=kLoop, calls=%fused_computation.117 | loop fusion | bytes 4194304 | tf_op jit(solution)/shard_map/slice | solution.py:185
  162.1 2.9 %copy.368 = bf16[1,1,4,2048,1,64]{3,5,2,4,1,0:T(8,128)(2,1)S(1)} copy(bf16[1,1,4,2048,1,64]{5,2,4,1,0,3:T(4,128)(2,1)} %get-tuple-element.19) | data formatting | bytes 2097152
  165.1 4.2 %copy.367 = bf16[1,1,4,2048,1,64]{3,5,2,4,1,0:T(8,128)(2,1)} copy(bf16[1,1,4,2048,1,64]{5,2,4,1,0,3:T(4,128)(2,1)} %get-tuple-element.18) | data formatting | bytes 2097152
  173.3 2.3 %divide_convert_fusion = bf16[1,4,512,64]{2,3,1,0:T(8,128)(2,1)S(1)} fusion(f32[1,4,512,64]{2,3,1,0:T(8,128)} %copy.339, f32[1,4,512,64]{2,3,1,0:T(8,128)} %copy.337, f32[1,4,512,64]{2,3,1,0:T(8,128)} %copy.336, f32[1,4,512,64]{2,3,1,0:T(8,128)} %copy.335, f32[1,4,512,64]{2,3,1,0:T(8,128)} %copy.332, f32[1,4,512,64]{2,3,1,0:T(8,128)} %reshape_broadcast_in_dim_reshape.9, ...), kind=kLoop, calls=%fused_computation.30 | loop fusion | flops 1703936 | bytes 3465216 | tf_op jit(solution)/shard_map/convert_element_type | solution.py:86
  176.5 2.2 %reduce.22 = bf16[512,256]{1,0:T(8,128)(2,1)S(1)} reduce(bf16[512,1,256]{2,1,0:T(2,128)(2,1)S(1)} %bitcast.215, bf16[]{:T(256)} %broadcast.472), dimensions={1}, to_apply=%bitcast.174.reduce_sub_computation | reduce | bytes 524290
  178.8 11.7 %all_to_all.15 = bf16[4,2,16384]{2,1,0:T(2,128)(2,1)S(1)} all-to-all(bf16[4,2,16384]{2,1,0:T(2,128)(2,1)S(1)} %reshape.1756), channel_id=1, replica_groups=mesh['seq'=64,'head'=4] {'head'}, dimensions={0} | all-to-all | bytes 524288 | tf_op jit(solution)/shard_map/all_to_all | solution.py:189
  (162 shorter events, 72.7 us)
Async XLA Ops:
  6.5 184.4 %copy-start = (bf16[1024,1024]{1,0:T(8,128)(2,1)S(1)}, bf16[1024,1024]{1,0:T(8,128)(2,1)}, u32[]{:S(2)}) copy-start(bf16[1024,1024]{1,0:T(8,128)(2,1)} %param.7) | copy-start | bytes 6291460
  6.5 151.2 %all-gather.3.cloned.1.call-start = ((), (), s32[]{:S(2)}) async-start(), calls=%async_computation.1 | async-start | bytes 4259840 | tf_op jit(solution)/shard_map/all_gather | solution.py:183
  9.2 44.7 %copy-start.1 = (bf16[1,512,256]{1,2,0:T(8,128)(2,1)}, bf16[1,512,256]{1,2,0:T(8,128)(2,1)S(1)}, u32[]{:S(2)}) copy-start(bf16[1,512,256]{1,2,0:T(8,128)(2,1)S(1)} %copy.286) | copy-start | bytes 786436
  24.6 18.3 %copy-start.13 = (bf16[1,512,256]{2,1,0:T(8,128)(2,1)S(1)}, bf16[1,512,256]{2,1,0:T(8,128)(2,1)}, u32[]{:S(2)}) copy-start(bf16[1,512,256]{2,1,0:T(8,128)(2,1)} %param.4) | copy-start | bytes 786436
  29.2 46.2 %collective-permute-start.5 = (bf16[2,1,4,32,64]{3,4,2,1,0:T(8,128)(2,1)}, bf16[2,1,4,32,64]{3,4,2,1,0:T(8,128)(2,1)}, u32[]{:S(2)}, u32[]{:S(2)}) collective-permute-start(bf16[2,1,4,32,64]{3,4,2,1,0:T(8,128)(2,1)} %bitcast.36), channel_id=1, source_target_pairs={{0,16},{16,0},{4,20},{20,4},{8,24},{24,8},{12,28},{28,12},{32,48},... | collective-permute-start | bytes 98312 | tf_op jit(solution)/shard_map/ppermute | solution.py:22
  32.9 61.1 %collective-permute-start.3 = (bf16[2,1,4,64,64]{3,4,2,1,0:T(8,128)(2,1)}, bf16[2,1,4,64,64]{3,4,2,1,0:T(8,128)(2,1)}, u32[]{:S(2)}, u32[]{:S(2)}) collective-permute-start(bf16[2,1,4,64,64]{3,4,2,1,0:T(8,128)(2,1)} %bitcast.32), channel_id=1, source_target_pairs={{0,8},{8,0},{4,12},{12,4},{16,24},{24,16},{20,28},{28,20},{32,40},... | collective-permute-start | bytes 196616 | tf_op jit(solution)/shard_map/ppermute | solution.py:22
  35.8 71.9 %collective-permute-start.2 = (bf16[2,1,4,128,64]{3,4,2,1,0:T(8,128)(2,1)}, bf16[2,1,4,128,64]{3,4,2,1,0:T(8,128)(2,1)}, u32[]{:S(2)}, u32[]{:S(2)}) collective-permute-start(bf16[2,1,4,128,64]{3,4,2,1,0:T(8,128)(2,1)} %bitcast.28), channel_id=1, source_target_pairs={{0,4},{4,0},{8,12},{12,8},{16,20},{20,16},{24,28},{28,24},{32,36},... | collective-permute-start | bytes 393224 | tf_op jit(solution)/shard_map/ppermute | solution.py:22
  37.0 77.2 %collective-permute-start.1 = (bf16[2,1,4,128,64]{3,4,2,1,0:T(8,128)(2,1)}, bf16[2,1,4,128,64]{3,4,2,1,0:T(8,128)(2,1)}, u32[]{:S(2)}, u32[]{:S(2)}) collective-permute-start(bf16[2,1,4,128,64]{3,4,2,1,0:T(8,128)(2,1)} %get-tuple-element.33), channel_id=1, source_target_pairs={{4,0},{8,4},{12,8},{16,12},{20,16},{24,20},{28,24},{32,28},{36,32}... | collective-permute-start | bytes 393224 | tf_op jit(solution)/shard_map/ppermute | solution.py:35
  38.2 75.9 %collective-permute-start = (bf16[2,1,4,128,64]{3,4,2,1,0:T(8,128)(2,1)}, bf16[2,1,4,128,64]{3,4,2,1,0:T(8,128)(2,1)}, u32[]{:S(2)}, u32[]{:S(2)}) collective-permute-start(bf16[2,1,4,128,64]{3,4,2,1,0:T(8,128)(2,1)} %get-tuple-element.32), channel_id=1, source_target_pairs={{0,4},{4,8},{8,12},{12,16},{16,20},{20,24},{24,28},{28,32},{32,36}... | collective-permute-start | bytes 393224 | tf_op jit(solution)/shard_map/ppermute | solution.py:33
  54.6 10.5 %copy-start.2 = (bf16[2,1,4,256,1,64]{5,4,3,2,1,0:T(2,128)(2,1)S(1)}, bf16[2,1,4,256,1,64]{5,4,3,2,1,0:T(2,128)(2,1)}, u32[]{:S(2)}) copy-start(bf16[2,1,4,256,1,64]{5,4,3,2,1,0:T(2,128)(2,1)} %get-tuple-element.17) | copy-start | bytes 786436
  61.6 10.6 %copy-start.9 = (bf16[1,4,128,1,64]{2,4,3,1,0:T(8,128)(2,1)}, bf16[1,4,128,1,64]{2,4,3,1,0:T(8,128)(2,1)S(1)}, u32[]{:S(2)}) copy-start(bf16[1,4,128,1,64]{2,4,3,1,0:T(8,128)(2,1)S(1)} %multiply_convert_fusion.4) | copy-start | bytes 196612
  75.4 13.1 %collective-permute-start.6 = (bf16[2,1,4,32,64]{3,4,2,1,0:T(8,128)(2,1)}, bf16[2,1,4,32,64]{3,4,2,1,0:T(8,128)(2,1)}, u32[]{:S(2)}, u32[]{:S(2)}) collective-permute-start(bf16[2,1,4,32,64]{3,4,2,1,0:T(8,128)(2,1)} %collective-permute-done.5), channel_id=1, source_target_pairs={{0,4},{4,0},{8,12},{12,8},{16,20},{20,16},{24,28},{28,24},{32,36},... | collective-permute-start | bytes 98312 | tf_op jit(solution)/shard_map/ppermute | solution.py:22
  89.8 6.6 %collective-permute-start.7 = (bf16[2,1,4,64,64]{3,4,2,1,0:T(8,128)(2,1)S(1)}, bf16[2,1,4,64,64]{3,4,2,1,0:T(8,128)(2,1)S(1)}, u32[]{:S(2)}, u32[]{:S(2)}) collective-permute-start(bf16[2,1,4,64,64]{3,4,2,1,0:T(8,128)(2,1)S(1)} %maximum_select_fusion.2), channel_id=1, source_target_pairs={{0,8},{8,0},{4,12},{12,4},{16,24},{24,16},{20,28},{28,20},{32,40},... | collective-permute-start | bytes 196616 | tf_op jit(solution)/shard_map/ppermute | solution.py:22
  94.0 7.8 %collective-permute-start.4 = (bf16[2,1,4,64,64]{3,4,2,1,0:T(8,128)(2,1)}, bf16[2,1,4,64,64]{3,4,2,1,0:T(8,128)(2,1)S(1)}, u32[]{:S(2)}, u32[]{:S(2)}) collective-permute-start(bf16[2,1,4,64,64]{3,4,2,1,0:T(8,128)(2,1)} %collective-permute-done.3), channel_id=1, source_target_pairs={{0,4},{4,0},{8,12},{12,8},{16,20},{20,16},{24,28},{28,24},{32,36},... | collective-permute-start | bytes 196616 | tf_op jit(solution)/shard_map/ppermute | solution.py:22
  97.6 0.6 copy-start.10
  97.6 0.6 copy-start.18
  108.9 0.7 copy-start.4
  116.3 8.4 %copy-start.3 = (bf16[4,4,128,64]{2,1,3,0:T(4,128)(2,1)S(1)}, bf16[4,4,128,64]{2,1,3,0:T(4,128)(2,1)}, u32[]{:S(2)}) copy-start(bf16[4,4,128,64]{2,1,3,0:T(4,128)(2,1)} %reshape.1717) | copy-start | bytes 786436
  123.3 3.9 %copy-start.20 = (pred[4,384]{1,0:T(4,128)(4,1)S(1)}, pred[4,384]{1,0:T(4,128)(4,1)}, u32[]{:S(2)}) copy-start(pred[4,384]{1,0:T(4,128)(4,1)} %pad_add_fusion) | copy-start | bytes 4612
  127.2 1.6 copy-start.6
  127.2 1.9 copy-start.7
  127.2 2.2 %copy-start.8 = (bf16[4,4,128,64]{2,1,3,0:T(4,128)(2,1)S(1)}, bf16[4,4,128,64]{2,1,3,0:T(4,128)(2,1)}, u32[]{:S(2)}) copy-start(bf16[4,4,128,64]{2,1,3,0:T(4,128)(2,1)} %reshape.1725) | copy-start | bytes 786436
  129.0 2.0 copy-start.11
  129.0 1.9 copy-start.19
  129.1 3.3 %copy-start.5 = (f32[4,128,128]{1,2,0:T(8,128)S(1)}, f32[4,128,128]{1,2,0:T(8,128)}, u32[]{:S(2)}) copy-start(f32[4,128,128]{1,2,0:T(8,128)} %copy-done.4) | copy-start | bytes 786436
  162.1 7.1 %copy-start.12 = (bf16[1,4,32,1,64]{4,3,2,1,0:T(2,128)(2,1)S(1)}, bf16[1,4,32,1,64]{4,3,2,1,0:T(2,128)(2,1)}, u32[]{:S(2)}) copy-start(bf16[1,4,32,1,64]{4,3,2,1,0:T(2,128)(2,1)} %fusion.32) | copy-start | bytes 49156
  170.8 2.4 %copy-start.14 = (f32[4,4,128]{2,1,0:T(4,128)S(1)}, f32[4,4,128]{2,1,0:T(4,128)}, u32[]{:S(2)}) copy-start(f32[4,4,128]{2,1,0:T(4,128)} %get-tuple-element.12) | copy-start | bytes 24580
  170.8 2.4 %copy-start.15 = (f32[4,512]{1,0:T(4,128)S(1)}, f32[4,512]{1,0:T(4,128)}, u32[]{:S(2)}) copy-start(f32[4,512]{1,0:T(4,128)} %copy.341) | copy-start | bytes 24580
  170.9 2.4 %copy-start.16 = (f32[4,512]{1,0:T(4,128)S(1)}, f32[4,512]{1,0:T(4,128)}, u32[]{:S(2)}) copy-start(f32[4,512]{1,0:T(4,128)} %copy.311) | copy-start | bytes 24580
  170.9 2.4 %copy-start.17 = (f32[4,512]{1,0:T(4,128)S(1)}, f32[4,512]{1,0:T(4,128)}, u32[]{:S(2)}) copy-start(f32[4,512]{1,0:T(4,128)} %broadcast_in_dim.151) | copy-start | bytes 24580
Sparse Core Ops, SparseCore 0:
  29.3 128.3 all-gather.2
where the time goes:
time: 201 us; the launch traced here: 199 us
  local copies, waits for them, and re-layouts  86.4 us (43%)
  other arithmetic  28.4 us (14%)
  waiting for transfers between devices  25.4 us (13%)
  starting transfers between devices  17.8 us (9%)
  matrix products  15.3 us (8%)
  between operations  14.1 us (7%)
  blocking collectives  11.7 us (6%)
    all_gather x1, waiting for transfers between devices, per_device(): summit = lax.all_gather(level_kv, 'seq', axis=3, tiled=True)  24.3 us
    unnamed x61, local copies, waits for them, and re-layouts  21.7 us
    broadcast_in_dim x10, local copies, waits for them, and re-layouts, combined(): jnp.repeat(record[2], 2 ** record[0], axis=2) * factor[..., None]  16.2 us
    ppermute x6, starting transfers between devices, swapped(): return lax.ppermute(block, axis, route)  11.9 us
    all_to_all x1, blocking collectives, per_device(): lax.all_to_all(attended, 'head', split_axis=1, concat_axis=2, tiled=True)  11.7 us
    another operation x7, local copies, waits for them, and re-layouts  9.28 us
    slice x5, local copies, waits for them, and re-layouts, pooled(): pairs[..., 1, :]  9.13 us
    convert_element_type x3, other arithmetic, pooled(): field.astype(jnp.float32)  7.3 us
  transfers between devices with their start and end apart: 9, of which 2 were waited for; matrix products, arithmetic and copies ran while one was open for 42% of the time, Pallas kernels for 0%

commit v1 on v0

v1 whole, which is shorter than its diff:
```python
import math

import jax
import jax.numpy as jnp
from jax import lax
from jax.experimental import pallas as pl
from jax.experimental.pallas import tpu as pltpu
from jax.sharding import PartitionSpec as P

HD = 64
BLOCK = 128
HEADS_HERE = 4
ROWS = 512
FEATURES = HEADS_HERE * HD
SLAB = HD + 16
SCALE = HD**-0.5 * math.log2(math.e)
MASKED = -1e30
BF16, F32 = jnp.bfloat16, jnp.float32
MESH = pl.DeviceIdType.MESH


def iota(shape, axis):
    return lax.broadcasted_iota(jnp.int32, shape, axis)


def dot(a, b):
    return jnp.dot(a, b, preferred_element_type=F32)


def dot_nt(a, b):
    return lax.dot_general(a, b, (((1,), (1,)), ((), ())), preferred_element_type=F32)


def rounded(value):
    return value.astype(BF16).astype(F32)


def split_top(top):
    high = rounded(top)
    return high, rounded(top - high)


def selector(rows, columns, shift, offset=0):
    hit = iota((rows, columns), 0) == offset + (iota((rows, columns), 1) >> shift)
    return jnp.where(hit, 1.0, 0.0).astype(BF16)


def pooler(level):
    rows = ROWS >> level
    hit = iota((rows, ROWS), 0) == (iota((rows, ROWS), 1) >> level)
    return jnp.where(hit, 1.0, 0.0).astype(BF16)


def kernel(
    q_hbm, k_hbm, v_hbm, w_hbm, o_ref,
    q_s, kx, vx, w_s,
    qn, q1m, q2m, q3m,
    k1, v1, kv2_s, kv2_r, kv3_s, kv3_r,
    vtn, vt1, vt2, vt3,
    s1, r1, kv_all, q_far, st, p_s, lhs_s, ret_s, ret_r,
    x1, x2, x3, x4, e1, e2, e3, e4,
    near, near_top, att_s, att_r,
    in_sem, halo_send, halo_recv, s1_send, s1_recv, l2_send, l2_recv, l3_send, l3_recv,
    kv_send, kv_recv, q_send, q_recv, own_send, own_recv, far_send, far_recv, a2a_send, a2a_recv,
):
    s, g = lax.axis_index("seq"), lax.axis_index("head")
    last = lax.axis_size("seq") - 1
    z, x, y = lax.div(s, 8), lax.rem(lax.div(s, 4), 2), lax.rem(s, 4)
    ring = s - y
    half = lax.div(z, 4) * 32
    place = lax.rem(z, 4) * 2 + x
    mirror = (7 - z) * 8 + x * 4

    def ring_peer(d):
        return ring + lax.rem(y + d, 4)

    def half_peer(d):
        n = lax.rem(place + d, 8)
        return half + n * 4 + y

    barrier = pltpu.get_barrier_semaphore()

    def greet(seq, head):
        pl.semaphore_signal(barrier, inc=1, device_id=(seq, head), device_id_type=MESH)

    for d in range(1, 4):
        greet(ring_peer(d), g)
    for d in range(1, 8):
        greet(half_peer(d), g)
    for j in range(4):
        greet(mirror + j, g)
    for d in range(1, 4):
        greet(s, lax.rem(g + d, 4))

    @pl.when(s > 0)
    def _():
        greet(s - 1, g)

    @pl.when(s < last)
    def _():
        greet(s + 1, g)

    loads = [
        pltpu.make_async_copy(k_hbm.at[0], kx.at[pl.ds(BLOCK, ROWS)], in_sem.at[0]),
        pltpu.make_async_copy(v_hbm.at[0], vx.at[pl.ds(BLOCK, ROWS)], in_sem.at[1]),
        pltpu.make_async_copy(q_hbm.at[0], q_s, in_sem.at[2]),
        pltpu.make_async_copy(w_hbm, w_s, in_sem.at[3]),
    ]
    for load in loads:
        load.start()

    lane = iota((32, 128), 1)
    low = lane < HD

    for load in loads[:3]:
        load.wait()
    own_k, own_v = kx.at[pl.ds(BLOCK, ROWS)], vx.at[pl.ds(BLOCK, ROWS)]
    pool4 = pooler(4)
    k4 = rounded(dot(pool4, own_k[...]) * 0.25)
    v4 = rounded(dot(pool4, own_v[...]) * 0.25)
    q4 = rounded(dot(pool4, q_s[...]) * 0.25)
    for h in range(HEADS_HERE):
        pair = slice(h // 2 * 128, h // 2 * 128 + 128)
        kp, vp, qp = k4[:, pair], v4[:, pair], q4[:, pair]
        if h % 2 == 0:
            packed = jnp.where(low, kp, pltpu.roll(vp, HD, 1))
        else:
            packed = jnp.where(low, pltpu.roll(kp, HD, 1), vp)
            qp = pltpu.roll(qp, HD, 1)
        s1[h, 0] = packed.astype(BF16)
        s1[h, 1] = jnp.where(low, qp, 0.0).astype(BF16)

    pl.semaphore_wait(
        barrier, 17 + jnp.where(s > 0, 1, 0) + jnp.where(s < last, 1, 0)
    )

    def remote(src, dst, send, recv, seq, head=None):
        return pltpu.make_async_remote_copy(
            src_ref=src, dst_ref=dst, send_sem=send, recv_sem=recv,
            device_id=(seq, g if head is None else head), device_id_type=MESH,
        )

    my_rows = pl.ds(pl.multiple_of(y * 32, 32), 32)
    ring_copies = [
        remote(
            s1.at[lax.rem(y + d, 4)], r1.at[:, my_rows, :],
            s1_send.at[d - 1], s1_recv.at[d - 1], ring_peer(d),
        )
        for d in range(1, 4)
    ]
    for copy in ring_copies:
        copy.start()
    r1[:, my_rows, :] = s1[y]

    def pool_pair(level, scale):
        pool = pooler(level)
        return dot(pool, own_k[...]) * scale, dot(pool, own_v[...]) * scale

    kp, vp = pool_pair(3, 0.5**1.5)
    kv3_s[0], kv3_s[1] = kp.astype(BF16), vp.astype(BF16)
    slot3 = pl.ds(pl.multiple_of(lax.rem(y, 2) * 64, 64), 64)
    pair3 = ring + (1 - lax.div(y, 2)) * 2
    l3_copies = [
        remote(kv3_s, kv3_r.at[:, slot3, :], l3_send.at[j], l3_recv.at[lax.rem(y, 2)], pair3 + j)
        for j in range(2)
    ]
    for copy in l3_copies:
        copy.start()
    kp, vp = pool_pair(2, 0.5)
    kv2_s[0], kv2_s[1] = kp.astype(BF16), vp.astype(BF16)
    l2_copy = remote(
        kv2_s, kv2_r, l2_send, l2_recv, s + 1 - 2 * lax.rem(y, 2)
    )
    l2_copy.start()

    head_rows, tail_rows = pl.ds(0, BLOCK), pl.ds(ROWS - BLOCK, BLOCK)
    to_left = [
        remote(k_hbm.at[0, head_rows], kx.at[pl.ds(BLOCK + ROWS, BLOCK)], halo_send.at[0], halo_recv.at[0], s - 1),
        remote(v_hbm.at[0, head_rows], vx.at[pl.ds(BLOCK + ROWS, BLOCK)], halo_send.at[1], halo_recv.at[1], s - 1),
    ]
    to_right = [
        remote(k_hbm.at[0, tail_rows], kx.at[pl.ds(0, BLOCK)], halo_send.at[2], halo_recv.at[2], s + 1),
        remote(v_hbm.at[0, tail_rows], vx.at[pl.ds(0, BLOCK)], halo_send.at[3], halo_recv.at[3], s + 1),
    ]

    @pl.when(s > 0)
    def _():
        for copy in to_left:
            copy.start()

    @pl.when(s < last)
    def _():
        for copy in to_right:
            copy.start()

    zeros = jnp.zeros((BLOCK, FEATURES), BF16)

    @pl.when(s == 0)
    def _():
        kx[0:BLOCK] = zeros
        vx[0:BLOCK] = zeros

    @pl.when(s == last)
    def _():
        kx[BLOCK + ROWS :] = zeros
        vx[BLOCK + ROWS :] = zeros

    for copy in ring_copies:
        copy.wait_recv()
    kv_all[place] = r1[0]
    half_copies = [
        remote(r1.at[0], kv_all.at[place], kv_send.at[d - 1], kv_recv.at[d - 1], half_peer(d))
        for d in range(1, 8)
    ]
    far_q = remote(r1.at[1], q_far, q_send, q_recv, mirror + y)
    far_q.start()
    for copy in half_copies:
        copy.start()

    lane_half = iota((1, 128), 1) < HD
    halves = [jnp.where(lane_half, 1.0, 0.0), jnp.where(lane_half, 0.0, 1.0)]

    def masked_queries(dst, field, count):
        for p in range(2):
            part = field[:, p * 128 : p * 128 + 128]
            for odd in range(2):
                dst[p, odd * count : (odd + 1) * count, :] = (part * halves[odd]).astype(BF16)

    for b in range(4):
        masked_queries(qn.at[b], q_s[b * BLOCK : (b + 1) * BLOCK, :].astype(F32), BLOCK)
    pooled_q = dot(pooler(1), q_s[...]) * 0.5**0.5
    for b in range(2):
        masked_queries(q1m.at[b], pooled_q[b * BLOCK : (b + 1) * BLOCK, :], BLOCK)
    masked_queries(q2m, dot(pooler(2), q_s[...]) * 0.5, BLOCK)
    masked_queries(q3m, dot(pooler(3), q_s[...]) * 0.5**1.5, 64)
    kp, vp = pool_pair(1, 0.5**0.5)
    k1[...] = kp.astype(BF16)
    v1[...] = vp.astype(BF16)

    ones16 = jnp.ones((16, BLOCK), BF16)

    def turn(dst, block, column):
        turned = block.T
        for h in range(HEADS_HERE):
            dst[h, 0:HD, column : column + BLOCK] = turned[h * HD : (h + 1) * HD, :]
            dst[h, HD:SLAB, column : column + BLOCK] = ones16

    for b in range(1, 5):
        turn(vtn, vx[b * BLOCK : (b + 1) * BLOCK, :], b * BLOCK)
    for b in range(2):
        turn(vt1, v1[b * BLOCK : (b + 1) * BLOCK, :], b * BLOCK)

    def attend(keys, queries, values, count, exact, biases=None):
        scores = [dot_nt(key, queries) for key in keys]
        if biases:
            scores = [a if bias is None else a + bias for a, bias in zip(scores, biases)]
        top = jnp.max(scores[0], axis=0, keepdims=True)
        for part in scores[1:]:
            top = jnp.maximum(top, jnp.max(part, axis=0, keepdims=True))
        top = top * SCALE
        high = below = None
        if not exact:
            high, below = split_top(top)
            top = high + below
        weights = [jnp.exp2(part * SCALE - top).astype(BF16) for part in scores]
        weights = weights[0] if len(weights) == 1 else jnp.concatenate(weights, axis=0)
        results = [
            dot(values[odd], weights[:, odd * count : (odd + 1) * count]) for odd in range(2)
        ]
        return top, high, below, results

    def near_block(b):
        for p in range(2):
            lanes = slice(p * 128, p * 128 + 128)
            keys = [kx[(b + i) * BLOCK : (b + i + 1) * BLOCK, lanes] for i in range(3)]
            values = [vtn[2 * p + odd, :, b * BLOCK : (b + 3) * BLOCK] for odd in range(2)]
            biases = [None, None, None]
            if b == 0:
                biases[0] = jnp.where(s == 0, MASKED, 0.0)
            if b == 3:
                biases[2] = jnp.where(s == last, MASKED, 0.0)
            top, _, _, results = attend(keys, qn[b, p], values, BLOCK, True, biases)
            columns = slice(b * BLOCK, (b + 1) * BLOCK)
            for odd in range(2):
                h = 2 * p + odd
                near[h, :, columns] = results[odd]
                near_top[h : h + 1, columns] = top[:, odd * BLOCK : (odd + 1) * BLOCK]

    def small_rows(count, high, below, total):
        row = iota((16, count), 0)
        total_high = rounded(total)
        rows = jnp.where(row == 2, total_high, total - total_high)
        rows = jnp.where(row == 1, below, rows)
        return jnp.where(row == 0, high, rows)

    def sibling(dst, keys, queries, values, count, column):
        for p in range(2):
            lanes = slice(p * 128, p * 128 + 128)
            _, high, below, results = attend(
                [keys[:, lanes]], queries[p], [values(2 * p), values(2 * p + 1)], count, False
            )
            for odd in range(2):
                h = 2 * p + odd
                own = slice(odd * count, (odd + 1) * count)
                columns = slice(column, column + count)
                dst[h * SLAB : h * SLAB + HD, columns] = results[odd][0:HD].astype(BF16)
                dst[h * SLAB + HD : (h + 1) * SLAB, columns] = small_rows(
                    count, high[:, own], below[:, own], results[odd][HD : HD + 1]
                ).astype(BF16)

    near_block(1)
    near_block(2)

    far_q.wait_recv()
    for copy in half_copies:
        copy.wait_recv()
    queries = jnp.concatenate([r1[1], q_far[...]], axis=0)
    full_low = iota((128, 128), 1) < HD
    top = None
    for j in range(8):
        block = kv_all[j]
        part = dot_nt(block, queries)
        st[j] = part
        part_top = jnp.max(part, axis=0, keepdims=True)
        top = part_top if top is None else jnp.maximum(top, part_top)
        turned = jnp.where(full_low, 1.0, block.astype(F32)).T
        lhs_s[:, j * 128 : (j + 1) * 128] = turned.astype(BF16)
    high, below = split_top(top * SCALE)
    top = high + below
    partner = place + 1 - 2 * x
    for j in range(8):
        weights = jnp.exp2(st[j] * SCALE - top)
        times = jnp.where(partner == j, 2.0, 1.0)
        p_s[j * 128 : (j + 1) * 128, 0:128] = (weights[:, 0:128] * times).astype(BF16)
        p_s[j * 128 : (j + 1) * 128, 128:256] = weights[:, 128:256].astype(BF16)
    result = dot(lhs_s[...], p_s[...])
    row = iota((128, 128), 0)
    for group in range(2):
        own = slice(group * 128, group * 128 + 128)
        part = result[:, own]
        total = part[4:5, :]
        total_high = rounded(total)
        part = jnp.where(row == 3, total - total_high, part)
        part = jnp.where(row == 2, total_high, part)
        part = jnp.where(row == 1, below[:, own], part)
        part = jnp.where(row == 0, high[:, own], part)
        ret_s[group] = part.T.astype(BF16)
    ret_copies = []
    for d in range(1, 4):
        there = pl.ds(pl.multiple_of(lax.rem(y + d, 4) * 32, 32), 32)
        ret_copies.append(
            remote(
                ret_s.at[0, there, :], ret_r.at[0, my_rows, :],
                own_send.at[d - 1], own_recv.at[d - 1], ring_peer(d),
            )
        )
    for j in range(4):
        ret_copies.append(
            remote(
                ret_s.at[1, pl.ds(j * 32, 32), :], ret_r.at[1, my_rows, :],
                far_send.at[j], far_recv.at[y], mirror + j,
            )
        )
    for copy in ret_copies:
        copy.start()
    ret_r[0, my_rows, :] = ret_s[0, my_rows, :]

    for b in range(2):
        other = 1 - b
        sibling(
            x1, k1[other * BLOCK : (other + 1) * BLOCK, :], q1m.at[b],
            lambda h, other=other: vt1[h, :, other * BLOCK : (other + 1) * BLOCK], BLOCK, b * BLOCK,
        )

    e1[...] = selector(256, ROWS, 1)
    e2[...] = selector(128, ROWS, 2)
    e3[...] = selector(64, ROWS, 3)
    for h in range(HEADS_HERE):
        e4[h] = selector(128, ROWS, 4, h * 32)

    for j in range(2):
        remote(kv3_s, kv3_r.at[:, pl.ds(j * 64, 64), :], l3_send.at[j], l3_recv.at[j], pair3 + j).wait_recv()
    turn(vt3, kv3_r[1], 0)
    sibling(x3, kv3_r[0], q3m, lambda h: vt3[h], 64, 0)
    l2_copy.wait_recv()
    turn(vt2, kv2_r[1], 0)
    sibling(x2, kv2_r[0], q2m, lambda h: vt2[h], BLOCK, 0)

    @pl.when(s > 0)
    def _():
        for copy in to_right:
            copy.wait_recv()

    turn(vtn, vx[0:BLOCK, :], 0)
    near_block(0)

    @pl.when(s < last)
    def _():
        for copy in to_left:
            copy.wait_recv()

    turn(vtn, vx[BLOCK + ROWS :, :], BLOCK + ROWS)
    near_block(3)

    for copy in ret_copies[:3]:
        copy.wait_recv()
    for j in range(4):
        remote(
            ret_s.at[1, pl.ds(j * 32, 32), :], ret_r.at[1, pl.ds(j * 32, 32), :],
            far_send.at[j], far_recv.at[j], mirror + j,
        ).wait_recv()
    parts = [ret_r[i].astype(F32).T for i in range(2)]
    tops = [part[0:1] + part[1:2] for part in parts]
    sums = [part[2:3] + part[3:4] for part in parts]
    top = jnp.maximum(tops[0], tops[1])
    factors = [jnp.exp2(t - top) for t in tops]
    high, below = split_top(top)
    x4[0:HD] = (parts[0][HD:] * factors[0] + parts[1][HD:] * factors[1]).astype(BF16)
    x4[HD:SLAB] = small_rows(
        128, high, below, sums[0] * factors[0] + sums[1] * factors[1]
    ).astype(BF16)

    a2a = []
    for d in (1, 2, 3, 0):
        target = lax.rem(g + d, 4)
        columns = pl.ds(pl.multiple_of(target * BLOCK, BLOCK), BLOCK)
        wide = [
            dot(field[...], select[:, columns])
            for field, select in ((x1, e1), (x2, e2), (x3, e3))
        ]
        for h in range(HEADS_HERE):
            terms = [part[h * SLAB : (h + 1) * SLAB] for part in wide]
            terms.append(dot(x4[...], e4[h, :, columns]))
            tops = [t[HD : HD + 1] + t[HD + 1 : HD + 2] for t in terms]
            sums = [t[HD + 2 : HD + 3] + t[HD + 3 : HD + 4] for t in terms]
            near_here = near[h, :, columns]
            tops.append(near_top[h : h + 1, columns])
            sums.append(near_here[HD : HD + 1])
            terms.append(near_here)
            top = tops[0]
            for other in tops[1:]:
                top = jnp.maximum(top, other)
            total = jnp.zeros((1, BLOCK), F32)
            factors = [jnp.exp2(t - top) for t in tops]
            for factor, part in zip(factors, sums):
                total = total + factor * part
            inverse = 1.0 / total
            mixed = jnp.zeros((HD, BLOCK), F32)
            for factor, part in zip(factors, terms):
                mixed = mixed + part[0:HD] * (factor * inverse)
            att_s[d, :, h * HD : (h + 1) * HD] = mixed.T.astype(BF16)
        if d:
            copy = remote(
                att_s.at[d], att_r.at[d], a2a_send.at[d - 1], a2a_recv.at[d - 1], s, target
            )
            copy.start()
            a2a.append(copy)

    loads[3].wait()

    def project(block, owner):
        return dot(block, w_s[pl.ds(pl.multiple_of(owner * FEATURES, FEATURES), FEATURES), :])

    total = project(att_s[0], g)
    for d in (1, 2, 3):
        a2a[d - 1].wait_recv()
        total = total + project(att_r[d], lax.rem(g + 4 - d, 4))
    o_ref[0] = total.astype(BF16)

    for copy in [*ring_copies, *l3_copies, l2_copy, far_q, *half_copies, *ret_copies, *a2a]:
        copy.wait_send()

    @pl.when(s > 0)
    def _():
        for copy in to_left:
            copy.wait_send()

    @pl.when(s < last)
    def _():
        for copy in to_right:
            copy.wait_send()


def per_device(queries, key_vectors, value_vectors, out_weight):
    def buf(*shape, dtype=BF16):
        return pltpu.VMEM(shape, dtype)

    dma = pltpu.SemaphoreType.DMA
    scratch = [
        buf(ROWS, 256), buf(768, 256), buf(768, 256), buf(1024, 1024),
        buf(4, 2, 256, 128), buf(2, 2, 256, 128), buf(2, 256, 128), buf(2, 128, 128),
        buf(256, 256), buf(256, 256), buf(2, 128, 256), buf(2, 128, 256), buf(2, 64, 256), buf(2, 128, 256),
        buf(4, SLAB, 768), buf(4, SLAB, 256), buf(4, SLAB, 128), buf(4, SLAB, 128),
        buf(4, 2, 32, 128), buf(2, 128, 128), buf(8, 128, 128), buf(128, 128),
        buf(8, 128, 256, dtype=F32), buf(1024, 256), buf(128, 1024), buf(2, 128, 128), buf(2, 128, 128),
        buf(4 * SLAB, 256), buf(4 * SLAB, 128), buf(4 * SLAB, 64), buf(SLAB, 128),
        buf(256, ROWS), buf(128, ROWS), buf(64, ROWS), buf(4, 128, ROWS),
        buf(4, SLAB, ROWS, dtype=F32), buf(8, ROWS, dtype=F32), buf(4, 128, 256), buf(4, 128, 256),
        dma((4,)), dma((4,)), dma((4,)), dma((3,)), dma((3,)), dma, dma, dma((2,)), dma((2,)),
        dma((7,)), dma((7,)), dma, dma, dma((3,)), dma((3,)), dma((4,)), dma((4,)), dma((3,)), dma((3,)),
    ]
    return pl.pallas_call(
        kernel,
        out_shape=jax.ShapeDtypeStruct((1, BLOCK, 1024), BF16),
        in_specs=[pl.BlockSpec(memory_space=pl.ANY)] * 4,
        out_specs=pl.BlockSpec(memory_space=pltpu.VMEM),
        scratch_shapes=scratch,
        compiler_params=pltpu.CompilerParams(
            collective_id=0, has_side_effects=True, vmem_limit_bytes=40 * 2**20
        ),
    )(queries, key_vectors, value_vectors, out_weight)


def solution(mesh):
    return jax.shard_map(
        per_device,
        mesh=mesh,
        in_specs=(P(None, "seq", "head"), P(None, "seq", "head"), P(None, "seq", "head"), P()),
        out_specs=P(None, ("seq", "head"), None),
        check_vma=False,
    )
```

time: 201 us -> 39.5 us (0.20)
  local copies, waits for them, and re-layouts: 86.4 us -> 5.14 us
  Pallas kernels: 0 us -> 34.1 us
  other arithmetic: 28.4 us -> 0 us
  waiting for transfers between devices: 25.4 us -> 0 us
  starting transfers between devices: 17.8 us -> 0 us
  matrix products: 15.3 us -> 0 us
  between operations: 14.1 us -> 0.01 us
  blocking collectives: 11.7 us -> 0 us
    pallas_call x0 -> x1, Pallas kernels: none -> 34.1 us  [per_device(): pl.pallas_call(kernel, out_shape=jax.ShapeDtypeStruct((1, BLOCK, 1024), B...]
    broadcast_in_dim x33 -> x0, local copies, waits for them, and re-layouts: 24.5 us -> none  [the longest x10 16.2 us: combined(): jnp.repeat(record[2], 2 ** record[0], axis=2) * factor[..., None]]
    all_gather x1 -> x0, waiting for transfers between devices: 24.3 us -> none  [per_device(): summit = lax.all_gather(level_kv, 'seq', axis=3, tiled=True)]
    slice x13 -> x0, local copies, waits for them, and re-layouts: 19.3 us -> none  [the longest x5 9.13 us: pooled(): pairs[..., 1, :]]
    ppermute x8 -> x0, starting transfers between devices: 17.8 us -> none  [the longest x6 11.9 us: swapped(): return lax.ppermute(block, axis, route)]
    unnamed x61 -> x9, local copies, waits for them, and re-layouts: 21.7 us -> 5.14 us
    convert_element_type x10 -> x0, other arithmetic: 15.4 us -> none  [the longest x3 7.3 us: pooled(): field.astype(jnp.float32)]
    dot_general x16 -> x0, matrix products: 14.1 us -> none  [the longest x5 6.11 us: attend(): jnp.einsum('shnqd,shnkd->shnqk', query_blocks, key_blocks, preferred_elem...]
  transfers between devices with their start and end apart: 9 -> 0, of which waited for: 2 -> 0; matrix products, arithmetic and copies ran while one was open for 42% -> 0% of each run, Pallas kernels for 0% -> 0%
where the time goes in v1:
time: 39.5 us; the launch traced here: 39.3 us
  Pallas kernels  34.1 us (86%)
  local copies, waits for them, and re-layouts  5.14 us (13%)
    pallas_call x1, Pallas kernels, per_device(): pl.pallas_call(kernel, out_shape=jax.ShapeDtypeStruct((1, BLOCK, 1024), B...  34.1 us
    unnamed x9, local copies, waits for them, and re-layouts  5.14 us

profile of v1, /device:TPU:1, one launch (start us, length us, event | category | flops | bytes accessed | tf_op | source)
XLA Modules:
  0.0 39.3 jit_solution(11902009334646221896)
XLA Ops:
  0.0 0.0 copy-start
  0.0 1.6 %copy-done = bf16[1024,1024]{1,0:T(8,128)(2,1)S(1)} copy-done((bf16[1024,1024]{1,0:T(8,128)(2,1)S(1)}, bf16[1024,1024]{1,0:T(8,128)(2,1)}, u32[]{:S(2)}) %copy-start) | copy-done | bytes 2097176
  1.6 0.0 copy-start.1
  1.6 0.9 %copy-done.1 = bf16[1,512,256]{2,1,0:T(8,128)(2,1)S(1)} copy-done((bf16[1,512,256]{2,1,0:T(8,128)(2,1)S(1)}, bf16[1,512,256]{2,1,0:T(8,128)(2,1)}, u32[]{:S(2)}) %copy-start.1) | copy-done | bytes 262168
  2.5 0.0 copy-start.2
  2.5 0.9 %copy-done.2 = bf16[1,512,256]{2,1,0:T(8,128)(2,1)S(1)} copy-done((bf16[1,512,256]{2,1,0:T(8,128)(2,1)S(1)}, bf16[1,512,256]{2,1,0:T(8,128)(2,1)}, u32[]{:S(2)}) %copy-start.2) | copy-done | bytes 262168
  3.5 0.0 copy-start.3
  3.5 0.9 %copy-done.3 = bf16[1,512,256]{2,1,0:T(8,128)(2,1)S(1)} copy-done((bf16[1,512,256]{2,1,0:T(8,128)(2,1)S(1)}, bf16[1,512,256]{2,1,0:T(8,128)(2,1)}, u32[]{:S(2)}) %copy-start.3) | copy-done | bytes 262168
  4.4 34.1 %shard_map.46 = bf16[1,128,1024]{2,1,0:T(8,128)(2,1)S(1)} custom-call(bf16[1,512,256]{2,1,0:T(8,128)(2,1)S(1)} %copy-done.1, bf16[1,512,256]{2,1,0:T(8,128)(2,1)S(1)} %copy-done.2, bf16[1,512,256]{2,1,0:T(8,128)(2,1)S(1)} %copy-done.3, bf16[1024,1024]{1,0:T(8,128)(2,1)S(1)} %copy-done), custom_call_target="tpu_custom_call" | custom-call | tf_op jit(solution)/shard_map/pallas_call | solution.py:502
  38.6 0.7 %copy.6 = bf16[1,128,1024]{2,1,0:T(8,128)(2,1)} copy(bf16[1,128,1024]{2,1,0:T(8,128)(2,1)S(1)} %shard_map.46) | data formatting | bytes 524288
Async XLA Ops:
  0.0 1.6 %copy-start = (bf16[1024,1024]{1,0:T(8,128)(2,1)S(1)}, bf16[1024,1024]{1,0:T(8,128)(2,1)}, u32[]{:S(2)}) copy-start(bf16[1024,1024]{1,0:T(8,128)(2,1)} %w_hbm.1) | copy-start | bytes 6291460
  1.6 0.9 %copy-start.1 = (bf16[1,512,256]{2,1,0:T(8,128)(2,1)S(1)}, bf16[1,512,256]{2,1,0:T(8,128)(2,1)}, u32[]{:S(2)}) copy-start(bf16[1,512,256]{2,1,0:T(8,128)(2,1)} %q_hbm.1) | copy-start | bytes 786436
  2.5 0.9 %copy-start.2 = (bf16[1,512,256]{2,1,0:T(8,128)(2,1)S(1)}, bf16[1,512,256]{2,1,0:T(8,128)(2,1)}, u32[]{:S(2)}) copy-start(bf16[1,512,256]{2,1,0:T(8,128)(2,1)} %k_hbm.1) | copy-start | bytes 786436
  3.5 0.9 %copy-start.3 = (bf16[1,512,256]{2,1,0:T(8,128)(2,1)S(1)}, bf16[1,512,256]{2,1,0:T(8,128)(2,1)}, u32[]{:S(2)}) copy-start(bf16[1,512,256]{2,1,0:T(8,128)(2,1)} %v_hbm.1) | copy-start | bytes 786436

commit v2 on v1

--- a/solution.py
+++ b/solution.py
@@ -57,48 +57,31 @@
     qn, q1m, q2m, q3m,
     k1, v1, kv2_s, kv2_r, kv3_s, kv3_r,
     vtn, vt1, vt2, vt3,
-    s1, r1, kv_all, q_far, st, p_s, lhs_s, ret_s, ret_r,
-    x1, x2, x3, x4, e1, e2, e3, e4,
-    near, near_top, att_s, att_r,
+    s1, r1, kv_all, q_far, ret_s, top_r,
+    x1, x2, x3, e1, e2, e3,
+    near, near_top, att_s, att_r, om_s, om_r, om_x, att_f,
     in_sem, halo_send, halo_recv, s1_send, s1_recv, l2_send, l2_recv, l3_send, l3_recv,
-    kv_send, kv_recv, q_send, q_recv, own_send, own_recv, far_send, far_recv, a2a_send, a2a_recv,
+    kv_send, kv_recv, q_send, q_recv, ret_send, ret_recv, a2a_send, a2a_recv, om_send, om_recv,
+    half_ready, mirror_ready,
 ):
     s, g = lax.axis_index("seq"), lax.axis_index("head")
     last = lax.axis_size("seq") - 1
     z, x, y = lax.div(s, 8), lax.rem(lax.div(s, 4), 2), lax.rem(s, 4)
     ring = s - y
+    zl = lax.rem(z, 4)
+    bit1, bit0 = lax.div(zl, 2), lax.rem(zl, 2)
     half = lax.div(z, 4) * 32
-    place = lax.rem(z, 4) * 2 + x
+    place = zl * 2 + x
     mirror = (7 - z) * 8 + x * 4
-
-    def ring_peer(d):
-        return ring + lax.rem(y + d, 4)
-
-    def half_peer(d):
-        n = lax.rem(place + d, 8)
-        return half + n * 4 + y
-
-    barrier = pltpu.get_barrier_semaphore()
-
-    def greet(seq, head):
-        pl.semaphore_signal(barrier, inc=1, device_id=(seq, head), device_id_type=MESH)
-
-    for d in range(1, 4):
-        greet(ring_peer(d), g)
-    for d in range(1, 8):
-        greet(half_peer(d), g)
-    for j in range(4):
-        greet(mirror + j, g)
-    for d in range(1, 4):
-        greet(s, lax.rem(g + d, 4))
-
-    @pl.when(s > 0)
-    def _():
-        greet(s - 1, g)
-
-    @pl.when(s < last)
-    def _():
-        greet(s + 1, g)
+    early, late = z < 4, z >= 4
+
+    def flipped(f):
+        high = 1 - bit1 if f & 4 else bit1
+        low = 1 - bit0 if f & 2 else bit0
+        return (high * 2 + low) * 2 + (1 - x if f & 1 else x)
+
+    def half_peer(f):
+        return half + flipped(f) * 4 + y
 
     loads = [
         pltpu.make_async_copy(k_hbm.at[0], kx.at[pl.ds(BLOCK, ROWS)], in_sem.at[0]),
@@ -109,29 +92,62 @@
     for load in loads:
         load.start()
 
-    lane = iota((32, 128), 1)
-    low = lane < HD
-
-    for load in loads[:3]:
-        load.wait()
+    barrier = pltpu.get_barrier_semaphore()
+
+    def signal(semaphore, seq, head):
+        pl.semaphore_signal(semaphore, inc=1, device_id=(seq, head), device_id_type=MESH)
+
+    for dy in range(4):
+        for dg in range(4):
+            if dy or dg:
+                signal(barrier, ring + lax.rem(y + dy, 4), lax.rem(g + dg, 4))
+    left_out = (y == 0) & (s > 0)
+    right_out = (y == 3) & (s < last)
+
+    @pl.when(left_out)
+    def _():
+        signal(barrier, s - 1, g)
+
+    @pl.when(right_out)
+    def _():
+        signal(barrier, s + 1, g)
+
+    @pl.when(early)
+    def _():
+        signal(barrier, mirror + y, g)
+
+    for f in range(1, 8):
+
+        @pl.when(late | (flipped(f) > place))
+        def _(f=f):
+            signal(barrier, half_peer(f), g)
+
+    low32 = iota((32, 128), 1) < HD
+
+    pool4 = pooler(4)
     own_k, own_v = kx.at[pl.ds(BLOCK, ROWS)], vx.at[pl.ds(BLOCK, ROWS)]
-    pool4 = pooler(4)
+    loads[0].wait()
     k4 = rounded(dot(pool4, own_k[...]) * 0.25)
+    loads[1].wait()
     v4 = rounded(dot(pool4, own_v[...]) * 0.25)
+    loads[2].wait()
     q4 = rounded(dot(pool4, q_s[...]) * 0.25)
     for h in range(HEADS_HERE):
         pair = slice(h // 2 * 128, h // 2 * 128 + 128)
         kp, vp, qp = k4[:, pair], v4[:, pair], q4[:, pair]
         if h % 2 == 0:
-            packed = jnp.where(low, kp, pltpu.roll(vp, HD, 1))
+            packed = jnp.where(low32, kp, pltpu.roll(vp, HD, 1))
         else:
-            packed = jnp.where(low, pltpu.roll(kp, HD, 1), vp)
+            packed = jnp.where(low32, pltpu.roll(kp, HD, 1), vp)
             qp = pltpu.roll(qp, HD, 1)
         s1[h, 0] = packed.astype(BF16)
-        s1[h, 1] = jnp.where(low, qp, 0.0).astype(BF16)
+        s1[h, 1] = jnp.where(low32, qp, 0.0).astype(BF16)
+    my_rows = pl.ds(pl.multiple_of(y * 32, 32), 32)
+    r1[:, my_rows, :] = s1[y]
 
     pl.semaphore_wait(
-        barrier, 17 + jnp.where(s > 0, 1, 0) + jnp.where(s < last, 1, 0)
+        barrier,
+        15 + jnp.where(left_out, 1, 0) + jnp.where(right_out, 1, 0) + jnp.where(late, 8, place),
     )
 
     def remote(src, dst, send, recv, seq, head=None):
@@ -140,17 +156,33 @@
             device_id=(seq, g if head is None else head), device_id_type=MESH,
         )
 
-    my_rows = pl.ds(pl.multiple_of(y * 32, 32), 32)
     ring_copies = [
         remote(
             s1.at[lax.rem(y + d, 4)], r1.at[:, my_rows, :],
-            s1_send.at[d - 1], s1_recv.at[d - 1], ring_peer(d),
+            s1_send.at[d - 1], s1_recv.at[d - 1], ring + lax.rem(y + d, 4),
         )
         for d in range(1, 4)
     ]
     for copy in ring_copies:
         copy.start()
-    r1[:, my_rows, :] = s1[y]
+
+    def forward(rows):
+        for f in range(1, 8):
+            remote(
+                r1.at[0, rows, :], kv_all.at[place, rows, :],
+                kv_send.at[f - 1], kv_recv.at[f - 1], half_peer(f),
+            ).start()
+
+    @pl.when(late)
+    def _():
+        forward(my_rows)
+        signal(mirror_ready, mirror + y, g)
+
+    for f in range(1, 8):
+
+        @pl.when(early & (flipped(f) < place))
+        def _(f=f):
+            signal(half_ready, half_peer(f), g)
 
     def pool_pair(level, scale):
         pool = pooler(level)
@@ -168,9 +200,7 @@
         copy.start()
     kp, vp = pool_pair(2, 0.5)
     kv2_s[0], kv2_s[1] = kp.astype(BF16), vp.astype(BF16)
-    l2_copy = remote(
-        kv2_s, kv2_r, l2_send, l2_recv, s + 1 - 2 * lax.rem(y, 2)
-    )
+    l2_copy = remote(kv2_s, kv2_r, l2_send, l2_recv, s + 1 - 2 * lax.rem(y, 2))
     l2_copy.start()
 
     head_rows, tail_rows = pl.ds(0, BLOCK), pl.ds(ROWS - BLOCK, BLOCK)
@@ -205,18 +235,6 @@
         kx[BLOCK + ROWS :] = zeros
         vx[BLOCK + ROWS :] = zeros
 
-    for copy in ring_copies:
-        copy.wait_recv()
-    kv_all[place] = r1[0]
-    half_copies = [
-        remote(r1.at[0], kv_all.at[place], kv_send.at[d - 1], kv_recv.at[d - 1], half_peer(d))
-        for d in range(1, 8)
-    ]
-    far_q = remote(r1.at[1], q_far, q_send, q_recv, mirror + y)
-    far_q.start()
-    for copy in half_copies:
-        copy.start()
-
     lane_half = iota((1, 128), 1) < HD
     halves = [jnp.where(lane_half, 1.0, 0.0), jnp.where(lane_half, 0.0, 1.0)]
 
@@ -228,14 +246,6 @@
 
     for b in range(4):
         masked_queries(qn.at[b], q_s[b * BLOCK : (b + 1) * BLOCK, :].astype(F32), BLOCK)
-    pooled_q = dot(pooler(1), q_s[...]) * 0.5**0.5
-    for b in range(2):
-        masked_queries(q1m.at[b], pooled_q[b * BLOCK : (b + 1) * BLOCK, :], BLOCK)
-    masked_queries(q2m, dot(pooler(2), q_s[...]) * 0.5, BLOCK)
-    masked_queries(q3m, dot(pooler(3), q_s[...]) * 0.5**1.5, 64)
-    kp, vp = pool_pair(1, 0.5**0.5)
-    k1[...] = kp.astype(BF16)
-    v1[...] = vp.astype(BF16)
 
     ones16 = jnp.ones((16, BLOCK), BF16)
 
@@ -247,8 +257,6 @@
 
     for b in range(1, 5):
         turn(vtn, vx[b * BLOCK : (b + 1) * BLOCK, :], b * BLOCK)
-    for b in range(2):
-        turn(vt1, v1[b * BLOCK : (b + 1) * BLOCK, :], b * BLOCK)
 
     def attend(keys, queries, values, count, exact, biases=None):
         scores = [dot_nt(key, queries) for key in keys]
@@ -309,74 +317,48 @@
                 ).astype(BF16)
 
     near_block(1)
+
+    far_q = remote(r1.at[1], q_far, q_send, q_recv, mirror + y)
+
+    @pl.when(late)
+    def _():
+        for d in (1, 3, 2):
+            ring_copies[d - 1].wait_recv()
+            rows = pl.ds(pl.multiple_of(lax.rem(y + 4 - d, 4) * 32, 32), 32)
+            forward(rows)
+        far_q.start()
+
     near_block(2)
-
-    far_q.wait_recv()
-    for copy in half_copies:
-        copy.wait_recv()
-    queries = jnp.concatenate([r1[1], q_far[...]], axis=0)
-    full_low = iota((128, 128), 1) < HD
-    top = None
-    for j in range(8):
-        block = kv_all[j]
-        part = dot_nt(block, queries)
-        st[j] = part
-        part_top = jnp.max(part, axis=0, keepdims=True)
-        top = part_top if top is None else jnp.maximum(top, part_top)
-        turned = jnp.where(full_low, 1.0, block.astype(F32)).T
-        lhs_s[:, j * 128 : (j + 1) * 128] = turned.astype(BF16)
-    high, below = split_top(top * SCALE)
-    top = high + below
-    partner = place + 1 - 2 * x
-    for j in range(8):
-        weights = jnp.exp2(st[j] * SCALE - top)
-        times = jnp.where(partner == j, 2.0, 1.0)
-        p_s[j * 128 : (j + 1) * 128, 0:128] = (weights[:, 0:128] * times).astype(BF16)
-        p_s[j * 128 : (j + 1) * 128, 128:256] = weights[:, 128:256].astype(BF16)
-    result = dot(lhs_s[...], p_s[...])
-    row = iota((128, 128), 0)
-    for group in range(2):
-        own = slice(group * 128, group * 128 + 128)
-        part = result[:, own]
-        total = part[4:5, :]
-        total_high = rounded(total)
-        part = jnp.where(row == 3, total - total_high, part)
-        part = jnp.where(row == 2, total_high, part)
-        part = jnp.where(row == 1, below[:, own], part)
-        part = jnp.where(row == 0, high[:, own], part)
-        ret_s[group] = part.T.astype(BF16)
-    ret_copies = []
-    for d in range(1, 4):
-        there = pl.ds(pl.multiple_of(lax.rem(y + d, 4) * 32, 32), 32)
-        ret_copies.append(
-            remote(
-                ret_s.at[0, there, :], ret_r.at[0, my_rows, :],
-                own_send.at[d - 1], own_recv.at[d - 1], ring_peer(d),
-            )
-        )
-    for j in range(4):
-        ret_copies.append(
-            remote(
-                ret_s.at[1, pl.ds(j * 32, 32), :], ret_r.at[1, my_rows, :],
-                far_send.at[j], far_recv.at[y], mirror + j,
-            )
-        )
-    for copy in ret_copies:
-        copy.start()
-    ret_r[0, my_rows, :] = ret_s[0, my_rows, :]
-
+    pooled_q = dot(pooler(1), q_s[...]) * 0.5**0.5
+    for b in range(2):
+        masked_queries(q1m.at[b], pooled_q[b * BLOCK : (b + 1) * BLOCK, :], BLOCK)
+    masked_queries(q2m, dot(pooler(2), q_s[...]) * 0.5, BLOCK)
+    masked_queries(q3m, dot(pooler(3), q_s[...]) * 0.5**1.5, 64)
+    kp, vp = pool_pair(1, 0.5**0.5)
+    k1[...] = kp.astype(BF16)
+    v1[...] = vp.astype(BF16)
+    for b in range(2):
+        turn(vt1, v1[b * BLOCK : (b + 1) * BLOCK, :], b * BLOCK)
     for b in range(2):
         other = 1 - b
         sibling(
             x1, k1[other * BLOCK : (other + 1) * BLOCK, :], q1m.at[b],
             lambda h, other=other: vt1[h, :, other * BLOCK : (other + 1) * BLOCK], BLOCK, b * BLOCK,
         )
-
     e1[...] = selector(256, ROWS, 1)
     e2[...] = selector(128, ROWS, 2)
     e3[...] = selector(64, ROWS, 3)
-    for h in range(HEADS_HERE):
-        e4[h] = selector(128, ROWS, 4, h * 32)
+
+    @pl.when(early)
+    def _():
+        for copy in ring_copies:
+            copy.wait_recv()
+
+        @pl.when(place < 7)
+        def _():
+            pl.semaphore_wait(half_ready, 7 - place)
+
+        forward(pl.ds(0, BLOCK))
 
     for j in range(2):
         remote(kv3_s, kv3_r.at[:, pl.ds(j * 64, 64), :], l3_send.at[j], l3_recv.at[j], pair3 + j).wait_recv()
@@ -402,23 +384,10 @@
     turn(vtn, vx[BLOCK + ROWS :, :], BLOCK + ROWS)
     near_block(3)
 
-    for copy in ret_copies[:3]:
-        copy.wait_recv()
-    for j in range(4):
-        remote(
-            ret_s.at[1, pl.ds(j * 32, 32), :], ret_r.at[1, pl.ds(j * 32, 32), :],
-            far_send.at[j], far_recv.at[j], mirror + j,
-        ).wait_recv()
-    parts = [ret_r[i].astype(F32).T for i in range(2)]
-    tops = [part[0:1] + part[1:2] for part in parts]
-    sums = [part[2:3] + part[3:4] for part in parts]
-    top = jnp.maximum(tops[0], tops[1])
-    factors = [jnp.exp2(t - top) for t in tops]
-    high, below = split_top(top)
-    x4[0:HD] = (parts[0][HD:] * factors[0] + parts[1][HD:] * factors[1]).astype(BF16)
-    x4[HD:SLAB] = small_rows(
-        128, high, below, sums[0] * factors[0] + sums[1] * factors[1]
-    ).astype(BF16)
+    @pl.when(early)
+    def _():
+        pl.semaphore_wait(mirror_ready, 1)
+        far_q.start()
 
     a2a = []
     for d in (1, 2, 3, 0):
@@ -428,9 +397,9 @@
             dot(field[...], select[:, columns])
             for field, select in ((x1, e1), (x2, e2), (x3, e3))
         ]
+        mixes, logs = [], []
         for h in range(HEADS_HERE):
             terms = [part[h * SLAB : (h + 1) * SLAB] for part in wide]
-            terms.append(dot(x4[...], e4[h, :, columns]))
             tops = [t[HD : HD + 1] + t[HD + 1 : HD + 2] for t in terms]
             sums = [t[HD + 2 : HD + 3] + t[HD + 3 : HD + 4] for t in terms]
             near_here = near[h, :, columns]
@@ -448,27 +417,124 @@
             mixed = jnp.zeros((HD, BLOCK), F32)
             for factor, part in zip(factors, terms):
                 mixed = mixed + part[0:HD] * (factor * inverse)
-            att_s[d, :, h * HD : (h + 1) * HD] = mixed.T.astype(BF16)
+            mixes.append(mixed)
+            logs.append(top + jnp.log2(total))
+        mixed = jnp.concatenate(mixes, axis=0).T.astype(BF16)
+        row = iota((8, BLOCK), 0)
+        rows = jnp.zeros((8, BLOCK), F32)
+        for h in range(HEADS_HERE):
+            rows = jnp.where(row == h, logs[h], rows)
         if d:
-            copy = remote(
-                att_s.at[d], att_r.at[d], a2a_send.at[d - 1], a2a_recv.at[d - 1], s, target
-            )
-            copy.start()
-            a2a.append(copy)
-
+            att_s[d - 1] = mixed
+            om_s[d - 1] = rows
+            pair = [
+                remote(att_s.at[d - 1], att_r.at[g], a2a_send.at[d - 1], a2a_recv.at[d - 1], s, target),
+                remote(om_s.at[d - 1], om_r.at[g], om_send.at[d - 1], om_recv.at[d - 1], s, target),
+            ]
+            for copy in pair:
+                copy.start()
+            a2a += pair
+        else:
+            att_r[g] = mixed
+            om_r[g] = rows
+
+    far_q.wait_recv()
+    queries = jnp.concatenate([r1[1], q_far[...]], axis=0)
+    low128 = iota((128, 128), 1) < HD
+    top = acc = None
+    for f in range(8):
+        if f:
+            remote(
+                r1.at[0], kv_all.at[flipped(f)], kv_send.at[f - 1], kv_recv.at[f - 1], half_peer(f)
+            ).wait_recv()
+        block = kv_all[flipped(f)] if f else r1[0]
+        scores = dot_nt(block, queries)
+        turned = jnp.where(low128, 1.0, block.astype(F32)).T.astype(BF16)
+        here = jnp.max(scores, axis=0, keepdims=True) * SCALE
+        high = here if f == 0 else jnp.maximum(top, here)
+        weights = jnp.exp2(scores * SCALE - high)
+        if f == 1:
+            weights = jnp.concatenate([weights[:, 0:128] * 2.0, weights[:, 128:256]], axis=1)
+        part = dot(turned, weights.astype(BF16))
+        acc = part if f == 0 else acc * jnp.exp2(top - high) + part
+        top = high
+    sums = acc[0:HD]
+    logs = top + jnp.log2(sums)
+    means = acc[HD:] / sums
+    odd_head = lax.rem(y, 2) == 1
+    result = jnp.concatenate(
+        [jnp.where(odd_head, logs, means), jnp.where(odd_head, means, logs)], axis=0
+    )
+    ret_s[...] = result.T
+    head_here = g * 4 + y
+
+    def give(slot, row, seq, head):
+        remote(
+            ret_s.at[pl.ds(pl.multiple_of(row, 8), 8), :], top_r.at[slot, head_here],
+            ret_send.at[slot], ret_recv.at[slot], seq, head,
+        ).start()
+
+    for j in range(4):
+        for t in range(4):
+            give(1, 128 + j * 32 + t * 8, mirror + j, t)
+    for dy in range(4):
+        for dg in range(4):
+            if dy or dg:
+                there, t = lax.rem(y + dy, 4), lax.rem(g + dg, 4)
+                give(0, there * 32 + t * 8, ring + there, t)
+    top_r[0, head_here] = ret_s[pl.ds(pl.multiple_of(y * 32 + g * 8, 8), 8), :]
+
+    for copy in a2a:
+        copy.wait_recv()
+    logs = om_r[...].reshape(32, BLOCK)
+    high = rounded(logs)
+    middle = rounded(logs - high)
+    lowest = rounded(logs - high - middle)
+    logs = jnp.concatenate([high, middle, lowest, jnp.zeros((32, BLOCK), F32)], axis=0)
+    k, c = iota((128, 1024), 0), iota((128, 1024), 1)
+    hit = ((k & 31) == ((c >> 8) * 8 + ((c >> 6) & 3))) & (k < 96)
+    spread = jnp.where(hit, 1.0, 0.0).astype(BF16)
+    om_x[...] = dot(logs.T.astype(BF16), spread)
     loads[3].wait()
 
-    def project(block, owner):
-        return dot(block, w_s[pl.ds(pl.multiple_of(owner * FEATURES, FEATURES), FEATURES), :])
-
-    total = project(att_s[0], g)
-    for d in (1, 2, 3):
-        a2a[d - 1].wait_recv()
-        total = total + project(att_r[d], lax.rem(g + 4 - d, 4))
-    o_ref[0] = total.astype(BF16)
-
-    for copy in [*ring_copies, *l3_copies, l2_copy, far_q, *half_copies, *ret_copies, *a2a]:
+    def arrived(slot, heads):
+        remote(
+            top_r.at[slot, pl.ds(0, heads)], top_r.at[slot, pl.ds(0, heads)],
+            ret_send.at[slot], ret_recv.at[slot], mirror + y,
+        ).wait_recv()
+
+    arrived(0, 15)
+    arrived(1, 16)
+    low8 = iota((8, 128), 1) < HD
+    for p in range(8):
+        means, logs = [], []
+        for slot in range(2):
+            even, odd = top_r[slot, 2 * p], top_r[slot, 2 * p + 1]
+            means.append(jnp.where(low8, even, odd))
+            logs.append(pltpu.roll(jnp.where(low8, odd, even), HD, 1))
+        top = jnp.maximum(logs[0], logs[1])
+        factors = [jnp.exp2(t - top) for t in logs]
+        total = factors[0] + factors[1]
+        mean = (means[0] * factors[0] + means[1] * factors[1]) / total
+        log = top + jnp.log2(total)
+        lanes = slice(p * 128, p * 128 + 128)
+        here = slice(p % 2 * 128, p % 2 * 128 + 128)
+        for q in range(8):
+            rows = slice(q * 16, q * 16 + 16)
+            other = att_r[p // 2, rows, here].astype(F32)
+            share = 1.0 / (1.0 + jnp.exp2(om_x[rows, lanes] - log[q : q + 1]))
+            att_f[rows, lanes] = (other + (mean[q : q + 1] - other) * share).astype(BF16)
+    o_ref[0] = dot(att_f[...], w_s[...]).astype(BF16)
+
+    for copy in [*ring_copies, *l3_copies, l2_copy, far_q, *a2a]:
         copy.wait_send()
+    for f in range(1, 8):
+        remote(r1.at[0], kv_all.at[place], kv_send.at[f - 1], kv_recv.at[f - 1], half_peer(f)).wait_send()
+    for slot, rows in ((0, 120), (1, 128)):
+        remote(
+            ret_s.at[pl.ds(0, rows)], ret_s.at[pl.ds(0, rows)],
+            ret_send.at[slot], ret_recv.at[slot], mirror + y,
+        ).wait_send()
 
     @pl.when(s > 0)
     def _():
@@ -486,27 +552,30 @@
         return pltpu.VMEM(shape, dtype)
 
     dma = pltpu.SemaphoreType.DMA
+    regular = pltpu.SemaphoreType.REGULAR
     scratch = [
         buf(ROWS, 256), buf(768, 256), buf(768, 256), buf(1024, 1024),
         buf(4, 2, 256, 128), buf(2, 2, 256, 128), buf(2, 256, 128), buf(2, 128, 128),
         buf(256, 256), buf(256, 256), buf(2, 128, 256), buf(2, 128, 256), buf(2, 64, 256), buf(2, 128, 256),
         buf(4, SLAB, 768), buf(4, SLAB, 256), buf(4, SLAB, 128), buf(4, SLAB, 128),
         buf(4, 2, 32, 128), buf(2, 128, 128), buf(8, 128, 128), buf(128, 128),
-        buf(8, 128, 256, dtype=F32), buf(1024, 256), buf(128, 1024), buf(2, 128, 128), buf(2, 128, 128),
-        buf(4 * SLAB, 256), buf(4 * SLAB, 128), buf(4 * SLAB, 64), buf(SLAB, 128),
-        buf(256, ROWS), buf(128, ROWS), buf(64, ROWS), buf(4, 128, ROWS),
-        buf(4, SLAB, ROWS, dtype=F32), buf(8, ROWS, dtype=F32), buf(4, 128, 256), buf(4, 128, 256),
+        buf(256, 128, dtype=F32), buf(2, 16, 8, 128, dtype=F32),
+        buf(4 * SLAB, 256), buf(4 * SLAB, 128), buf(4 * SLAB, 64),
+        buf(256, ROWS), buf(128, ROWS), buf(64, ROWS),
+        buf(4, SLAB, ROWS, dtype=F32), buf(8, ROWS, dtype=F32), buf(3, 128, 256), buf(4, 128, 256),
+        buf(3, 8, 128, dtype=F32), buf(4, 8, 128, dtype=F32), buf(128, 1024, dtype=F32), buf(128, 1024),
         dma((4,)), dma((4,)), dma((4,)), dma((3,)), dma((3,)), dma, dma, dma((2,)), dma((2,)),
-        dma((7,)), dma((7,)), dma, dma, dma((3,)), dma((3,)), dma((4,)), dma((4,)), dma((3,)), dma((3,)),
+        dma((7,)), dma((7,)), dma, dma, dma((2,)), dma((2,)), dma((3,)), dma((3,)), dma((3,)), dma((3,)),
+        regular, regular,
     ]
     return pl.pallas_call(
         kernel,
-        out_shape=jax.ShapeDtypeStruct((1, BLOCK, 1024), BF16),
+        out_shape=pltpu.VMEM((1, BLOCK, 1024), BF16),
         in_specs=[pl.BlockSpec(memory_space=pl.ANY)] * 4,
         out_specs=pl.BlockSpec(memory_space=pltpu.VMEM),
         scratch_shapes=scratch,
         compiler_params=pltpu.CompilerParams(
-            collective_id=0, has_side_effects=True, vmem_limit_bytes=40 * 2**20
+            collective_id=0, has_side_effects=True, vmem_limit_bytes=58 * 2**20
         ),
     )(queries, key_vectors, value_vectors, out_weight)
 

time: 39.5 us -> 33.4 us (0.85)
  local copies, waits for them, and re-layouts: 5.14 us -> 0.71 us
  Pallas kernels: 34.1 us -> 32.6 us
    unnamed x9 -> x1, local copies, waits for them, and re-layouts: 5.14 us -> 0.71 us
    pallas_call x1, Pallas kernels: 34.1 us -> 32.6 us  [per_device(): pl.pallas_call(kernel, out_shape=pltpu.VMEM((1, BLOCK, 1024), BF16), in_s...]
where the time goes in v2:
time: 33.4 us; the launch traced here: 33.3 us
  Pallas kernels  32.6 us (98%)
  local copies, waits for them, and re-layouts  0.71 us (2%)
    pallas_call x1, Pallas kernels, per_device(): pl.pallas_call(kernel, out_shape=pltpu.VMEM((1, BLOCK, 1024), BF16), in_s...  32.6 us
    unnamed x1, local copies, waits for them, and re-layouts  0.71 us

profile of v2, /device:TPU:1, one launch (start us, length us, event | category | flops | bytes accessed | tf_op | source)
XLA Modules:
  0.0 33.3 jit_solution(6779416431067835129)
XLA Ops:
  0.0 32.6 %shard_map.46 = bf16[1,128,1024]{2,1,0:T(8,128)(2,1)S(1)} custom-call(bf16[1,512,256]{2,1,0:T(8,128)(2,1)} %q_hbm.1, bf16[1,512,256]{2,1,0:T(8,128)(2,1)} %k_hbm.1, bf16[1,512,256]{2,1,0:T(8,128)(2,1)} %v_hbm.1, bf16[1024,1024]{1,0:T(8,128)(2,1)} %w_hbm.1), custom_call_target="tpu_custom_call" | custom-call | tf_op jit(solution)/shard_map/pallas_call | solution.py:571
  32.6 0.7 %copy.6 = bf16[1,128,1024]{2,1,0:T(8,128)(2,1)} copy(bf16[1,128,1024]{2,1,0:T(8,128)(2,1)S(1)} %shard_map.46) | data formatting | bytes 524288

commit v3 on v2

--- a/solution.py
+++ b/solution.py
@@ -61,27 +61,24 @@
     x1, x2, x3, e1, e2, e3,
     near, near_top, att_s, att_r, om_s, om_r, om_x, att_f,
     in_sem, halo_send, halo_recv, s1_send, s1_recv, l2_send, l2_recv, l3_send, l3_recv,
-    kv_send, kv_recv, q_send, q_recv, ret_send, ret_recv, a2a_send, a2a_recv, om_send, om_recv,
-    half_ready, mirror_ready,
+    kv_send, direct_send, kv_recv, q_send, q_recv, ret_send, ret_recv, a2a_send, a2a_recv, om_send, om_recv,
+    chain_up, chain_down, late_in,
 ):
     s, g = lax.axis_index("seq"), lax.axis_index("head")
     last = lax.axis_size("seq") - 1
     z, x, y = lax.div(s, 8), lax.rem(lax.div(s, 4), 2), lax.rem(s, 4)
     ring = s - y
     zl = lax.rem(z, 4)
-    bit1, bit0 = lax.div(zl, 2), lax.rem(zl, 2)
-    half = lax.div(z, 4) * 32
-    place = zl * 2 + x
-    mirror = (7 - z) * 8 + x * 4
+    bits = [lax.rem(z, 2), lax.rem(lax.div(z, 2), 2), lax.div(z, 4)]
+    mirror = z * 8 + (1 - x) * 4
     early, late = z < 4, z >= 4
 
     def flipped(f):
-        high = 1 - bit1 if f & 4 else bit1
-        low = 1 - bit0 if f & 2 else bit0
-        return (high * 2 + low) * 2 + (1 - x if f & 1 else x)
-
-    def half_peer(f):
-        return half + flipped(f) * 4 + y
+        low, middle, high = [1 - bit if f >> i & 1 else bit for i, bit in enumerate(bits)]
+        return high * 4 + middle * 2 + low
+
+    def column(other):
+        return other * 8 + x * 4
 
     loads = [
         pltpu.make_async_copy(k_hbm.at[0], kx.at[pl.ds(BLOCK, ROWS)], in_sem.at[0]),
@@ -97,30 +94,34 @@
     def signal(semaphore, seq, head):
         pl.semaphore_signal(semaphore, inc=1, device_id=(seq, head), device_id_type=MESH)
 
-    for dy in range(4):
-        for dg in range(4):
-            if dy or dg:
-                signal(barrier, ring + lax.rem(y + dy, 4), lax.rem(g + dg, 4))
-    left_out = (y == 0) & (s > 0)
-    right_out = (y == 3) & (s < last)
-
-    @pl.when(left_out)
+    ring_start, ring_end = (y == 0) & (s > 0), (y == 3) & (s < last)
+
+    @pl.when(early)
+    def _():
+        for other in range(4, 8):
+            for j in range(4):
+                signal(barrier, column(other) + j, g)
+
+    @pl.when(ring_start)
     def _():
         signal(barrier, s - 1, g)
 
-    @pl.when(right_out)
+    @pl.when(ring_end)
     def _():
         signal(barrier, s + 1, g)
 
-    @pl.when(early)
-    def _():
-        signal(barrier, mirror + y, g)
-
-    for f in range(1, 8):
-
-        @pl.when(late | (flipped(f) > place))
-        def _(f=f):
-            signal(barrier, half_peer(f), g)
+    for d in range(1, 4):
+        signal(barrier, ring + lax.rem(y + d, 4), g)
+        signal(barrier, s, lax.rem(g + d, 4))
+    signal(barrier, mirror + y, g)
+
+    @pl.when(zl < 3)
+    def _():
+        signal(barrier, s + 8, g)
+
+    @pl.when(zl > 0)
+    def _():
+        signal(barrier, s - 8, g)
 
     low32 = iota((32, 128), 1) < HD
 
@@ -147,7 +148,12 @@
 
     pl.semaphore_wait(
         barrier,
-        15 + jnp.where(left_out, 1, 0) + jnp.where(right_out, 1, 0) + jnp.where(late, 8, place),
+        7
+        + jnp.where(late, 16, 0)
+        + jnp.where(zl > 0, 1, 0)
+        + jnp.where(zl < 3, 1, 0)
+        + jnp.where(ring_start, 1, 0)
+        + jnp.where(ring_end, 1, 0),
     )
 
     def remote(src, dst, send, recv, seq, head=None):
@@ -163,46 +169,6 @@
         )
         for d in range(1, 4)
     ]
-    for copy in ring_copies:
-        copy.start()
-
-    def forward(rows):
-        for f in range(1, 8):
-            remote(
-                r1.at[0, rows, :], kv_all.at[place, rows, :],
-                kv_send.at[f - 1], kv_recv.at[f - 1], half_peer(f),
-            ).start()
-
-    @pl.when(late)
-    def _():
-        forward(my_rows)
-        signal(mirror_ready, mirror + y, g)
-
-    for f in range(1, 8):
-
-        @pl.when(early & (flipped(f) < place))
-        def _(f=f):
-            signal(half_ready, half_peer(f), g)
-
-    def pool_pair(level, scale):
-        pool = pooler(level)
-        return dot(pool, own_k[...]) * scale, dot(pool, own_v[...]) * scale
-
-    kp, vp = pool_pair(3, 0.5**1.5)
-    kv3_s[0], kv3_s[1] = kp.astype(BF16), vp.astype(BF16)
-    slot3 = pl.ds(pl.multiple_of(lax.rem(y, 2) * 64, 64), 64)
-    pair3 = ring + (1 - lax.div(y, 2)) * 2
-    l3_copies = [
-        remote(kv3_s, kv3_r.at[:, slot3, :], l3_send.at[j], l3_recv.at[lax.rem(y, 2)], pair3 + j)
-        for j in range(2)
-    ]
-    for copy in l3_copies:
-        copy.start()
-    kp, vp = pool_pair(2, 0.5)
-    kv2_s[0], kv2_s[1] = kp.astype(BF16), vp.astype(BF16)
-    l2_copy = remote(kv2_s, kv2_r, l2_send, l2_recv, s + 1 - 2 * lax.rem(y, 2))
-    l2_copy.start()
-
     head_rows, tail_rows = pl.ds(0, BLOCK), pl.ds(ROWS - BLOCK, BLOCK)
     to_left = [
         remote(k_hbm.at[0, head_rows], kx.at[pl.ds(BLOCK + ROWS, BLOCK)], halo_send.at[0], halo_recv.at[0], s - 1),
@@ -212,6 +178,8 @@
         remote(k_hbm.at[0, tail_rows], kx.at[pl.ds(0, BLOCK)], halo_send.at[2], halo_recv.at[2], s + 1),
         remote(v_hbm.at[0, tail_rows], vx.at[pl.ds(0, BLOCK)], halo_send.at[3], halo_recv.at[3], s + 1),
     ]
+    for copy in ring_copies:
+        copy.start()
 
     @pl.when(s > 0)
     def _():
@@ -222,6 +190,45 @@
     def _():
         for copy in to_right:
             copy.start()
+
+    @pl.when(zl == 1)
+    def _():
+        signal(chain_up, s + 8, g)
+
+    @pl.when(zl == 2)
+    def _():
+        signal(chain_down, s - 8, g)
+
+    @pl.when(late)
+    def _():
+        for i in range(4):
+            h = lax.rem(y + i, 4)
+            for other in range(4):
+                remote(
+                    s1.at[h, 0], kv_all.at[z, my_rows, :], direct_send, kv_recv.at[z],
+                    column(other) + h,
+                ).start()
+        for other in range(4):
+            signal(late_in, column(other) + y, g)
+
+    def pool_pair(level, scale):
+        pool = pooler(level)
+        return dot(pool, own_k[...]) * scale, dot(pool, own_v[...]) * scale
+
+    kp, vp = pool_pair(3, 0.5**1.5)
+    kv3_s[0], kv3_s[1] = kp.astype(BF16), vp.astype(BF16)
+    kp, vp = pool_pair(2, 0.5)
+    kv2_s[0], kv2_s[1] = kp.astype(BF16), vp.astype(BF16)
+
+    slot3 = pl.ds(pl.multiple_of(lax.rem(y, 2) * 64, 64), 64)
+    pair3 = ring + (1 - lax.div(y, 2)) * 2
+    l3_copies = [
+        remote(kv3_s, kv3_r.at[:, slot3, :], l3_send.at[j], l3_recv.at[lax.rem(y, 2)], pair3 + j)
+        for j in range(2)
+    ]
+    l2_copy = remote(kv2_s, kv2_r, l2_send, l2_recv, s + 1 - 2 * lax.rem(y, 2))
+    for copy in [*l3_copies, l2_copy]:
+        copy.start()
 
     zeros = jnp.zeros((BLOCK, FEATURES), BF16)
 
@@ -317,16 +324,21 @@
                 ).astype(BF16)
 
     near_block(1)
-
-    far_q = remote(r1.at[1], q_far, q_send, q_recv, mirror + y)
-
-    @pl.when(late)
-    def _():
-        for d in (1, 3, 2):
-            ring_copies[d - 1].wait_recv()
-            rows = pl.ds(pl.multiple_of(lax.rem(y + 4 - d, 4) * 32, 32), 32)
-            forward(rows)
-        far_q.start()
+    @pl.when(zl <= 1)
+    def _():
+        pl.semaphore_wait(chain_down, 1)
+
+    @pl.when(zl >= 2)
+    def _():
+        pl.semaphore_wait(chain_up, 1)
+
+    @pl.when(zl == 1)
+    def _():
+        signal(chain_down, s - 8, g)
+
+    @pl.when(zl == 2)
+    def _():
+        signal(chain_up, s + 8, g)
 
     near_block(2)
     pooled_q = dot(pooler(1), q_s[...]) * 0.5**0.5
@@ -349,46 +361,49 @@
     e2[...] = selector(128, ROWS, 2)
     e3[...] = selector(64, ROWS, 3)
 
+    far_q = remote(r1.at[1], q_far, q_send, q_recv, mirror + y)
+    for copy in ring_copies:
+        copy.wait_recv()
+    far_q.start()
+
+    def forward(f):
+        return remote(
+            r1.at[0], kv_all.at[z], kv_send.at[f - 1], kv_recv.at[z], column(flipped(f)) + y
+        )
+
+    for f in range(1, 4):
+        forward(f).start()
+
+    @pl.when(s > 0)
+    def _():
+        for copy in to_right:
+            copy.wait_recv()
+
+    turn(vtn, vx[0:BLOCK, :], 0)
+    near_block(0)
+
+    @pl.when(s < last)
+    def _():
+        for copy in to_left:
+            copy.wait_recv()
+
+    turn(vtn, vx[BLOCK + ROWS :, :], BLOCK + ROWS)
+    near_block(3)
+
     @pl.when(early)
     def _():
-        for copy in ring_copies:
-            copy.wait_recv()
-
-        @pl.when(place < 7)
-        def _():
-            pl.semaphore_wait(half_ready, 7 - place)
-
-        forward(pl.ds(0, BLOCK))
+        pl.semaphore_wait(late_in, 4)
+        for f in range(4, 8):
+            forward(f).start()
+
+    l2_copy.wait_recv()
+    turn(vt2, kv2_r[1], 0)
+    sibling(x2, kv2_r[0], q2m, lambda h: vt2[h], BLOCK, 0)
 
     for j in range(2):
         remote(kv3_s, kv3_r.at[:, pl.ds(j * 64, 64), :], l3_send.at[j], l3_recv.at[j], pair3 + j).wait_recv()
     turn(vt3, kv3_r[1], 0)
     sibling(x3, kv3_r[0], q3m, lambda h: vt3[h], 64, 0)
-    l2_copy.wait_recv()
-    turn(vt2, kv2_r[1], 0)
-    sibling(x2, kv2_r[0], q2m, lambda h: vt2[h], BLOCK, 0)
-
-    @pl.when(s > 0)
-    def _():
-        for copy in to_right:
-            copy.wait_recv()
-
-    turn(vtn, vx[0:BLOCK, :], 0)
-    near_block(0)
-
-    @pl.when(s < last)
-    def _():
-        for copy in to_left:
-            copy.wait_recv()
-
-    turn(vtn, vx[BLOCK + ROWS :, :], BLOCK + ROWS)
-    near_block(3)
-
-    @pl.when(early)
-    def _():
-        pl.semaphore_wait(mirror_ready, 1)
-        far_q.start()
-
     a2a = []
     for d in (1, 2, 3, 0):
         target = lax.rem(g + d, 4)
@@ -442,10 +457,11 @@
     queries = jnp.concatenate([r1[1], q_far[...]], axis=0)
     low128 = iota((128, 128), 1) < HD
     top = acc = None
-    for f in range(8):
+    for f in (0, 1, 2, 3, 7, 6, 5, 4):
         if f:
+            other = flipped(f)
             remote(
-                r1.at[0], kv_all.at[flipped(f)], kv_send.at[f - 1], kv_recv.at[f - 1], half_peer(f)
+                kv_all.at[other], kv_all.at[other], kv_send.at[f - 1], kv_recv.at[other], column(other) + y
             ).wait_recv()
         block = kv_all[flipped(f)] if f else r1[0]
         scores = dot_nt(block, queries)
@@ -453,8 +469,8 @@
         here = jnp.max(scores, axis=0, keepdims=True) * SCALE
         high = here if f == 0 else jnp.maximum(top, here)
         weights = jnp.exp2(scores * SCALE - high)
-        if f == 1:
-            weights = jnp.concatenate([weights[:, 0:128] * 2.0, weights[:, 128:256]], axis=1)
+        if f == 0:
+            weights = jnp.concatenate([weights[:, 0:128], weights[:, 128:256] * 2.0], axis=1)
         part = dot(turned, weights.astype(BF16))
         acc = part if f == 0 else acc * jnp.exp2(top - high) + part
         top = high
@@ -528,8 +544,18 @@
 
     for copy in [*ring_copies, *l3_copies, l2_copy, far_q, *a2a]:
         copy.wait_send()
-    for f in range(1, 8):
-        remote(r1.at[0], kv_all.at[place], kv_send.at[f - 1], kv_recv.at[f - 1], half_peer(f)).wait_send()
+    for f in range(1, 4):
+        forward(f).wait_send()
+
+    @pl.when(early)
+    def _():
+        for f in range(4, 8):
+            forward(f).wait_send()
+
+    @pl.when(late)
+    def _():
+        remote(kv_all.at[0:4], kv_all.at[0:4], direct_send, kv_recv.at[z], mirror + y).wait_send()
+
     for slot, rows in ((0, 120), (1, 128)):
         remote(
             ret_s.at[pl.ds(0, rows)], ret_s.at[pl.ds(0, rows)],
@@ -565,8 +591,8 @@
         buf(4, SLAB, ROWS, dtype=F32), buf(8, ROWS, dtype=F32), buf(3, 128, 256), buf(4, 128, 256),
         buf(3, 8, 128, dtype=F32), buf(4, 8, 128, dtype=F32), buf(128, 1024, dtype=F32), buf(128, 1024),
         dma((4,)), dma((4,)), dma((4,)), dma((3,)), dma((3,)), dma, dma, dma((2,)), dma((2,)),
-        dma((7,)), dma((7,)), dma, dma, dma((2,)), dma((2,)), dma((3,)), dma((3,)), dma((3,)), dma((3,)),
-        regular, regular,
+        dma((7,)), dma, dma((8,)), dma, dma, dma((2,)), dma((2,)), dma((3,)), dma((3,)), dma((3,)), dma((3,)),
+        regular, regular, regular,
     ]
     return pl.pallas_call(
         kernel,

time: 33.4 us -> 30 us (0.90)
  Pallas kernels: 32.6 us -> 29.2 us
    pallas_call x1, Pallas kernels: 32.6 us -> 29.2 us  [per_device(): pl.pallas_call(kernel, out_shape=pltpu.VMEM((1, BLOCK, 1024), BF16), in_s...]
where the time goes in v3:
time: 30 us; the launch traced here: 29.9 us
  Pallas kernels  29.2 us (97%)
  local copies, waits for them, and re-layouts  0.71 us (2%)
    pallas_call x1, Pallas kernels, per_device(): pl.pallas_call(kernel, out_shape=pltpu.VMEM((1, BLOCK, 1024), BF16), in_s...  29.2 us
    unnamed x1, local copies, waits for them, and re-layouts  0.71 us

profile of v3, /device:TPU:1, one launch (start us, length us, event | category | flops | bytes accessed | tf_op | source)
XLA Modules:
  0.0 29.9 jit_solution(9521877263351744379)
XLA Ops:
  0.0 29.2 %shard_map.46 = bf16[1,128,1024]{2,1,0:T(8,128)(2,1)S(1)} custom-call(bf16[1,512,256]{2,1,0:T(8,128)(2,1)} %q_hbm.1, bf16[1,512,256]{2,1,0:T(8,128)(2,1)} %k_hbm.1, bf16[1,512,256]{2,1,0:T(8,128)(2,1)} %v_hbm.1, bf16[1024,1024]{1,0:T(8,128)(2,1)} %w_hbm.1), custom_call_target="tpu_custom_call" | custom-call | tf_op jit(solution)/shard_map/pallas_call | solution.py:597
  29.2 0.7 %copy.6 = bf16[1,128,1024]{2,1,0:T(8,128)(2,1)} copy(bf16[1,128,1024]{2,1,0:T(8,128)(2,1)S(1)} %shard_map.46) | data formatting | bytes 524288

commit v4 on v3

--- a/solution.py
+++ b/solution.py
@@ -181,16 +181,6 @@
     for copy in ring_copies:
         copy.start()
 
-    @pl.when(s > 0)
-    def _():
-        for copy in to_left:
-            copy.start()
-
-    @pl.when(s < last)
-    def _():
-        for copy in to_right:
-            copy.start()
-
     @pl.when(zl == 1)
     def _():
         signal(chain_up, s + 8, g)
@@ -323,23 +313,17 @@
                     count, high[:, own], below[:, own], results[odd][HD : HD + 1]
                 ).astype(BF16)
 
+    @pl.when(s > 0)
+    def _():
+        for copy in to_left:
+            copy.start()
+
+    @pl.when(s < last)
+    def _():
+        for copy in to_right:
+            copy.start()
+
     near_block(1)
-    @pl.when(zl <= 1)
-    def _():
-        pl.semaphore_wait(chain_down, 1)
-
-    @pl.when(zl >= 2)
-    def _():
-        pl.semaphore_wait(chain_up, 1)
-
-    @pl.when(zl == 1)
-    def _():
-        signal(chain_down, s - 8, g)
-
-    @pl.when(zl == 2)
-    def _():
-        signal(chain_up, s + 8, g)
-
     near_block(2)
     pooled_q = dot(pooler(1), q_s[...]) * 0.5**0.5
     for b in range(2):
@@ -361,6 +345,22 @@
     e2[...] = selector(128, ROWS, 2)
     e3[...] = selector(64, ROWS, 3)
 
+    @pl.when(zl <= 1)
+    def _():
+        pl.semaphore_wait(chain_down, 1)
+
+    @pl.when(zl >= 2)
+    def _():
+        pl.semaphore_wait(chain_up, 1)
+
+    @pl.when(zl == 1)
+    def _():
+        signal(chain_down, s - 8, g)
+
+    @pl.when(zl == 2)
+    def _():
+        signal(chain_up, s + 8, g)
+
     far_q = remote(r1.at[1], q_far, q_send, q_recv, mirror + y)
     for copy in ring_copies:
         copy.wait_recv()
@@ -374,21 +374,72 @@
     for f in range(1, 4):
         forward(f).start()
 
-    @pl.when(s > 0)
-    def _():
-        for copy in to_right:
-            copy.wait_recv()
-
-    turn(vtn, vx[0:BLOCK, :], 0)
-    near_block(0)
-
-    @pl.when(s < last)
-    def _():
-        for copy in to_left:
-            copy.wait_recv()
-
-    turn(vtn, vx[BLOCK + ROWS :, :], BLOCK + ROWS)
-    near_block(3)
+    a2a = []
+    for d in range(1, 4):
+        a2a += [
+            remote(att_s.at[d - 1], att_r.at[g], a2a_send.at[d - 1], a2a_recv.at[d - 1], s, lax.rem(g + d, 4)),
+            remote(om_s.at[d - 1], om_r.at[g], om_send.at[d - 1], om_recv.at[d - 1], s, lax.rem(g + d, 4)),
+        ]
+
+    def rest():
+        @pl.when(s > 0)
+        def _():
+            for copy in to_right:
+                copy.wait_recv()
+
+        @pl.when(s < last)
+        def _():
+            for copy in to_left:
+                copy.wait_recv()
+
+        turn(vtn, vx[0:BLOCK, :], 0)
+        near_block(0)
+
+        turn(vtn, vx[BLOCK + ROWS :, :], BLOCK + ROWS)
+        near_block(3)
+
+        for d in (1, 2, 3, 0):
+            target = lax.rem(g + d, 4)
+            columns = pl.ds(pl.multiple_of(target * BLOCK, BLOCK), BLOCK)
+            wide = [
+                dot(field[...], select[:, columns])
+                for field, select in ((x1, e1), (x2, e2), (x3, e3))
+            ]
+            mixes, logs = [], []
+            for h in range(HEADS_HERE):
+                terms = [part[h * SLAB : (h + 1) * SLAB] for part in wide]
+                tops = [t[HD : HD + 1] + t[HD + 1 : HD + 2] for t in terms]
+                sums = [t[HD + 2 : HD + 3] + t[HD + 3 : HD + 4] for t in terms]
+                near_here = near[h, :, columns]
+                tops.append(near_top[h : h + 1, columns])
+                sums.append(near_here[HD : HD + 1])
+                terms.append(near_here)
+                top = tops[0]
+                for other in tops[1:]:
+                    top = jnp.maximum(top, other)
+                total = jnp.zeros((1, BLOCK), F32)
+                factors = [jnp.exp2(t - top) for t in tops]
+                for factor, part in zip(factors, sums):
+                    total = total + factor * part
+                inverse = 1.0 / total
+                mixed = jnp.zeros((HD, BLOCK), F32)
+                for factor, part in zip(factors, terms):
+                    mixed = mixed + part[0:HD] * (factor * inverse)
+                mixes.append(mixed)
+                logs.append(top + jnp.log2(total))
+            mixed = jnp.concatenate(mixes, axis=0).T.astype(BF16)
+            row = iota((8, BLOCK), 0)
+            rows = jnp.zeros((8, BLOCK), F32)
+            for h in range(HEADS_HERE):
+                rows = jnp.where(row == h, logs[h], rows)
+            if d:
+                att_s[d - 1] = mixed
+                om_s[d - 1] = rows
+                for copy in a2a[2 * d - 2 : 2 * d]:
+                    copy.start()
+            else:
+                att_r[g] = mixed
+                om_r[g] = rows
 
     @pl.when(early)
     def _():
@@ -397,72 +448,27 @@
             forward(f).start()
 
     l2_copy.wait_recv()
+    for j in range(2):
+        remote(kv3_s, kv3_r.at[:, pl.ds(j * 64, 64), :], l3_send.at[j], l3_recv.at[j], pair3 + j).wait_recv()
     turn(vt2, kv2_r[1], 0)
     sibling(x2, kv2_r[0], q2m, lambda h: vt2[h], BLOCK, 0)
 
-    for j in range(2):
-        remote(kv3_s, kv3_r.at[:, pl.ds(j * 64, 64), :], l3_send.at[j], l3_recv.at[j], pair3 + j).wait_recv()
     turn(vt3, kv3_r[1], 0)
     sibling(x3, kv3_r[0], q3m, lambda h: vt3[h], 64, 0)
-    a2a = []
-    for d in (1, 2, 3, 0):
-        target = lax.rem(g + d, 4)
-        columns = pl.ds(pl.multiple_of(target * BLOCK, BLOCK), BLOCK)
-        wide = [
-            dot(field[...], select[:, columns])
-            for field, select in ((x1, e1), (x2, e2), (x3, e3))
-        ]
-        mixes, logs = [], []
-        for h in range(HEADS_HERE):
-            terms = [part[h * SLAB : (h + 1) * SLAB] for part in wide]
-            tops = [t[HD : HD + 1] + t[HD + 1 : HD + 2] for t in terms]
-            sums = [t[HD + 2 : HD + 3] + t[HD + 3 : HD + 4] for t in terms]
-            near_here = near[h, :, columns]
-            tops.append(near_top[h : h + 1, columns])
-            sums.append(near_here[HD : HD + 1])
-            terms.append(near_here)
-            top = tops[0]
-            for other in tops[1:]:
-                top = jnp.maximum(top, other)
-            total = jnp.zeros((1, BLOCK), F32)
-            factors = [jnp.exp2(t - top) for t in tops]
-            for factor, part in zip(factors, sums):
-                total = total + factor * part
-            inverse = 1.0 / total
-            mixed = jnp.zeros((HD, BLOCK), F32)
-            for factor, part in zip(factors, terms):
-                mixed = mixed + part[0:HD] * (factor * inverse)
-            mixes.append(mixed)
-            logs.append(top + jnp.log2(total))
-        mixed = jnp.concatenate(mixes, axis=0).T.astype(BF16)
-        row = iota((8, BLOCK), 0)
-        rows = jnp.zeros((8, BLOCK), F32)
-        for h in range(HEADS_HERE):
-            rows = jnp.where(row == h, logs[h], rows)
-        if d:
-            att_s[d - 1] = mixed
-            om_s[d - 1] = rows
-            pair = [
-                remote(att_s.at[d - 1], att_r.at[g], a2a_send.at[d - 1], a2a_recv.at[d - 1], s, target),
-                remote(om_s.at[d - 1], om_r.at[g], om_send.at[d - 1], om_recv.at[d - 1], s, target),
-            ]
-            for copy in pair:
-                copy.start()
-            a2a += pair
-        else:
-            att_r[g] = mixed
-            om_r[g] = rows
+    @pl.when(z < 3)
+    def _():
+        rest()
 
     far_q.wait_recv()
+    for f in range(1, 8):
+        other = flipped(f)
+        remote(
+            kv_all.at[other], kv_all.at[other], kv_send.at[f - 1], kv_recv.at[other], column(other) + y
+        ).wait_recv()
     queries = jnp.concatenate([r1[1], q_far[...]], axis=0)
     low128 = iota((128, 128), 1) < HD
     top = acc = None
     for f in (0, 1, 2, 3, 7, 6, 5, 4):
-        if f:
-            other = flipped(f)
-            remote(
-                kv_all.at[other], kv_all.at[other], kv_send.at[f - 1], kv_recv.at[other], column(other) + y
-            ).wait_recv()
         block = kv_all[flipped(f)] if f else r1[0]
         scores = dot_nt(block, queries)
         turned = jnp.where(low128, 1.0, block.astype(F32)).T.astype(BF16)
@@ -499,6 +505,10 @@
                 there, t = lax.rem(y + dy, 4), lax.rem(g + dg, 4)
                 give(0, there * 32 + t * 8, ring + there, t)
     top_r[0, head_here] = ret_s[pl.ds(pl.multiple_of(y * 32 + g * 8, 8), 8), :]
+
+    @pl.when(z >= 3)
+    def _():
+        rest()
 
     for copy in a2a:
         copy.wait_recv()

time: 30 us -> 28 us (0.933)
  Pallas kernels: 29.2 us -> 27.2 us
    pallas_call x1, Pallas kernels: 29.2 us -> 27.2 us  [per_device(): pl.pallas_call(kernel, out_shape=pltpu.VMEM((1, BLOCK, 1024), BF16), in_s...]
where the time goes in v4:
time: 28 us; the launch traced here: 27.9 us
  Pallas kernels  27.2 us (97%)
  local copies, waits for them, and re-layouts  0.71 us (3%)
    pallas_call x1, Pallas kernels, per_device(): pl.pallas_call(kernel, out_shape=pltpu.VMEM((1, BLOCK, 1024), BF16), in_s...  27.2 us
    unnamed x1, local copies, waits for them, and re-layouts  0.71 us

profile of v4, /device:TPU:1, one launch (start us, length us, event | category | flops | bytes accessed | tf_op | source)
XLA Modules:
  0.0 27.9 jit_solution(14410655604545876862)
XLA Ops:
  0.0 27.2 %shard_map.46 = bf16[1,128,1024]{2,1,0:T(8,128)(2,1)S(1)} custom-call(bf16[1,512,256]{2,1,0:T(8,128)(2,1)} %q_hbm.1, bf16[1,512,256]{2,1,0:T(8,128)(2,1)} %k_hbm.1, bf16[1,512,256]{2,1,0:T(8,128)(2,1)} %v_hbm.1, bf16[1024,1024]{1,0:T(8,128)(2,1)} %w_hbm.1), custom_call_target="tpu_custom_call" | custom-call | tf_op jit(solution)/shard_map/pallas_call | solution.py:607
  27.2 0.7 %copy.6 = bf16[1,128,1024]{2,1,0:T(8,128)(2,1)} copy(bf16[1,128,1024]{2,1,0:T(8,128)(2,1)S(1)} %shard_map.46) | data formatting | bytes 524288

commit v5 on v4

--- a/solution.py
+++ b/solution.py
@@ -313,12 +313,14 @@
                     count, high[:, own], below[:, own], results[odd][HD : HD + 1]
                 ).astype(BF16)
 
-    @pl.when(s > 0)
+    calm = (z < 3) | (z > 3)
+
+    @pl.when((s > 0) & (calm | (y > 0)))
     def _():
         for copy in to_left:
             copy.start()
 
-    @pl.when(s < last)
+    @pl.when((s < last) & (calm | (y < 3)))
     def _():
         for copy in to_right:
             copy.start()
@@ -374,33 +376,39 @@
     for f in range(1, 4):
         forward(f).start()
 
-    a2a = []
-    for d in range(1, 4):
-        a2a += [
-            remote(att_s.at[d - 1], att_r.at[g], a2a_send.at[d - 1], a2a_recv.at[d - 1], s, lax.rem(g + d, 4)),
-            remote(om_s.at[d - 1], om_r.at[g], om_send.at[d - 1], om_recv.at[d - 1], s, lax.rem(g + d, 4)),
+    @pl.when(ring_start & (z == 3))
+    def _():
+        for copy in to_left:
+            copy.start()
+
+    @pl.when(ring_end & (z == 3))
+    def _():
+        for copy in to_right:
+            copy.start()
+
+    @pl.when(early)
+    def _():
+        pl.semaphore_wait(late_in, 4)
+        for f in range(4, 8):
+            forward(f).start()
+
+    l2_copy.wait_recv()
+    for j in range(2):
+        remote(kv3_s, kv3_r.at[:, pl.ds(j * 64, 64), :], l3_send.at[j], l3_recv.at[j], pair3 + j).wait_recv()
+    turn(vt2, kv2_r[1], 0)
+    sibling(x2, kv2_r[0], q2m, lambda h: vt2[h], BLOCK, 0)
+
+    turn(vt3, kv3_r[1], 0)
+    sibling(x3, kv3_r[0], q3m, lambda h: vt3[h], 64, 0)
+    def a2a(block, owner):
+        return [
+            remote(att_s.at[block], att_r.at[owner], a2a_send.at[block], a2a_recv.at[owner], s, block),
+            remote(om_s.at[block], om_r.at[owner], om_send.at[block], om_recv.at[owner], s, block),
         ]
 
-    def rest():
-        @pl.when(s > 0)
-        def _():
-            for copy in to_right:
-                copy.wait_recv()
-
-        @pl.when(s < last)
-        def _():
-            for copy in to_left:
-                copy.wait_recv()
-
-        turn(vtn, vx[0:BLOCK, :], 0)
-        near_block(0)
-
-        turn(vtn, vx[BLOCK + ROWS :, :], BLOCK + ROWS)
-        near_block(3)
-
-        for d in (1, 2, 3, 0):
-            target = lax.rem(g + d, 4)
-            columns = pl.ds(pl.multiple_of(target * BLOCK, BLOCK), BLOCK)
+    def combine(blocks):
+        for block in blocks:
+            columns = slice(block * BLOCK, (block + 1) * BLOCK)
             wide = [
                 dot(field[...], select[:, columns])
                 for field, select in ((x1, e1), (x2, e2), (x3, e3))
@@ -432,30 +440,41 @@
             rows = jnp.zeros((8, BLOCK), F32)
             for h in range(HEADS_HERE):
                 rows = jnp.where(row == h, logs[h], rows)
-            if d:
-                att_s[d - 1] = mixed
-                om_s[d - 1] = rows
-                for copy in a2a[2 * d - 2 : 2 * d]:
+            att_s[block] = mixed
+            om_s[block] = rows
+        for block in blocks:
+
+            @pl.when(g == block)
+            def _(block=block):
+                att_r[g] = att_s[block]
+                om_r[g] = om_s[block]
+
+            @pl.when(g != block)
+            def _(block=block):
+                for copy in a2a(block, g):
                     copy.start()
-            else:
-                att_r[g] = mixed
-                om_r[g] = rows
-
-    @pl.when(early)
-    def _():
-        pl.semaphore_wait(late_in, 4)
-        for f in range(4, 8):
-            forward(f).start()
-
-    l2_copy.wait_recv()
-    for j in range(2):
-        remote(kv3_s, kv3_r.at[:, pl.ds(j * 64, 64), :], l3_send.at[j], l3_recv.at[j], pair3 + j).wait_recv()
-    turn(vt2, kv2_r[1], 0)
-    sibling(x2, kv2_r[0], q2m, lambda h: vt2[h], BLOCK, 0)
-
-    turn(vt3, kv3_r[1], 0)
-    sibling(x3, kv3_r[0], q3m, lambda h: vt3[h], 64, 0)
-    @pl.when(z < 3)
+
+    combine((1, 2))
+
+    def rest():
+        @pl.when(s > 0)
+        def _():
+            for copy in to_right:
+                copy.wait_recv()
+
+        @pl.when(s < last)
+        def _():
+            for copy in to_left:
+                copy.wait_recv()
+
+        turn(vtn, vx[0:BLOCK, :], 0)
+        near_block(0)
+
+        turn(vtn, vx[BLOCK + ROWS :, :], BLOCK + ROWS)
+        near_block(3)
+        combine((0, 3))
+
+    @pl.when(z < 2)
     def _():
         rest()
 
@@ -506,12 +525,13 @@
                 give(0, there * 32 + t * 8, ring + there, t)
     top_r[0, head_here] = ret_s[pl.ds(pl.multiple_of(y * 32 + g * 8, 8), 8), :]
 
-    @pl.when(z >= 3)
+    @pl.when(z >= 2)
     def _():
         rest()
 
-    for copy in a2a:
-        copy.wait_recv()
+    for d in range(1, 4):
+        for copy in a2a(0, lax.rem(g + d, 4)):
+            copy.wait_recv()
     logs = om_r[...].reshape(32, BLOCK)
     high = rounded(logs)
     middle = rounded(logs - high)
@@ -552,8 +572,15 @@
             att_f[rows, lanes] = (other + (mean[q : q + 1] - other) * share).astype(BF16)
     o_ref[0] = dot(att_f[...], w_s[...]).astype(BF16)
 
-    for copy in [*ring_copies, *l3_copies, l2_copy, far_q, *a2a]:
+    for copy in [*ring_copies, *l3_copies, l2_copy, far_q]:
         copy.wait_send()
+    for block in range(4):
+
+        @pl.when(g != block)
+        def _(block=block):
+            for copy in a2a(block, g):
+                copy.wait_send()
+
     for f in range(1, 4):
         forward(f).wait_send()
 
@@ -598,10 +625,10 @@
         buf(256, 128, dtype=F32), buf(2, 16, 8, 128, dtype=F32),
         buf(4 * SLAB, 256), buf(4 * SLAB, 128), buf(4 * SLAB, 64),
         buf(256, ROWS), buf(128, ROWS), buf(64, ROWS),
-        buf(4, SLAB, ROWS, dtype=F32), buf(8, ROWS, dtype=F32), buf(3, 128, 256), buf(4, 128, 256),
-        buf(3, 8, 128, dtype=F32), buf(4, 8, 128, dtype=F32), buf(128, 1024, dtype=F32), buf(128, 1024),
+        buf(4, SLAB, ROWS, dtype=F32), buf(8, ROWS, dtype=F32), buf(4, 128, 256), buf(4, 128, 256),
+        buf(4, 8, 128, dtype=F32), buf(4, 8, 128, dtype=F32), buf(128, 1024, dtype=F32), buf(128, 1024),
         dma((4,)), dma((4,)), dma((4,)), dma((3,)), dma((3,)), dma, dma, dma((2,)), dma((2,)),
-        dma((7,)), dma, dma((8,)), dma, dma, dma((2,)), dma((2,)), dma((3,)), dma((3,)), dma((3,)), dma((3,)),
+        dma((7,)), dma, dma((8,)), dma, dma, dma((2,)), dma((2,)), dma((4,)), dma((4,)), dma((4,)), dma((4,)),
         regular, regular, regular,
     ]
     return pl.pallas_call(

time: 28 us -> 26.9 us (0.961)
  Pallas kernels: 27.2 us -> 26 us
    pallas_call x1, Pallas kernels: 27.2 us -> 26 us  [per_device(): pl.pallas_call(kernel, out_shape=pltpu.VMEM((1, BLOCK, 1024), BF16), in_s...]
where the time goes in v5:
time: 26.9 us; the launch traced here: 26.7 us
  Pallas kernels  26 us (97%)
  local copies, waits for them, and re-layouts  0.71 us (3%)
    pallas_call x1, Pallas kernels, per_device(): pl.pallas_call(kernel, out_shape=pltpu.VMEM((1, BLOCK, 1024), BF16), in_s...  26 us
    unnamed x1, local copies, waits for them, and re-layouts  0.71 us

profile of v5, /device:TPU:1, one launch (start us, length us, event | category | flops | bytes accessed | tf_op | source)
XLA Modules:
  0.0 26.7 jit_solution(3071039494861792366)
XLA Ops:
  0.0 26.0 %shard_map.46 = bf16[1,128,1024]{2,1,0:T(8,128)(2,1)S(1)} custom-call(bf16[1,512,256]{2,1,0:T(8,128)(2,1)} %q_hbm.1, bf16[1,512,256]{2,1,0:T(8,128)(2,1)} %k_hbm.1, bf16[1,512,256]{2,1,0:T(8,128)(2,1)} %v_hbm.1, bf16[1024,1024]{1,0:T(8,128)(2,1)} %w_hbm.1), custom_call_target="tpu_custom_call" | custom-call | tf_op jit(solution)/shard_map/pallas_call | solution.py:634
  26.0 0.7 %copy.6 = bf16[1,128,1024]{2,1,0:T(8,128)(2,1)} copy(bf16[1,128,1024]{2,1,0:T(8,128)(2,1)S(1)} %shard_map.46) | data formatting | bytes 524288

commit v6 on v5

--- a/solution.py
+++ b/solution.py
@@ -373,7 +373,7 @@
             r1.at[0], kv_all.at[z], kv_send.at[f - 1], kv_recv.at[z], column(flipped(f)) + y
         )
 
-    for f in range(1, 4):
+    for f in (3, 2, 1):
         forward(f).start()
 
     @pl.when(ring_start & (z == 3))
@@ -435,7 +435,7 @@
                     mixed = mixed + part[0:HD] * (factor * inverse)
                 mixes.append(mixed)
                 logs.append(top + jnp.log2(total))
-            mixed = jnp.concatenate(mixes, axis=0).T.astype(BF16)
+            mixed = jnp.concatenate(mixes, axis=0).astype(BF16).T
             row = iota((8, BLOCK), 0)
             rows = jnp.zeros((8, BLOCK), F32)
             for h in range(HEADS_HERE):
@@ -479,18 +479,24 @@
         rest()
 
     far_q.wait_recv()
-    for f in range(1, 8):
+    def arrive(f):
         other = flipped(f)
         remote(
             kv_all.at[other], kv_all.at[other], kv_send.at[f - 1], kv_recv.at[other], column(other) + y
         ).wait_recv()
+
+    for f in (1, 2, 5, 6, 7):
+        arrive(f)
     queries = jnp.concatenate([r1[1], q_far[...]], axis=0)
-    low128 = iota((128, 128), 1) < HD
+    ones64 = jnp.ones((HD, 128), BF16)
     top = acc = None
-    for f in (0, 1, 2, 3, 7, 6, 5, 4):
+    for f in (0, 1, 2, 7, 6, 5, 3, 4):
+        if f == 3:
+            for late_block in (3, 4,):
+                arrive(late_block)
         block = kv_all[flipped(f)] if f else r1[0]
         scores = dot_nt(block, queries)
-        turned = jnp.where(low128, 1.0, block.astype(F32)).T.astype(BF16)
+        turned = jnp.concatenate([ones64, block.T[HD:]], axis=0)
         here = jnp.max(scores, axis=0, keepdims=True) * SCALE
         high = here if f == 0 else jnp.maximum(top, here)
         weights = jnp.exp2(scores * SCALE - high)

time: 26.9 us -> 26.9 us (level)
  no operation moved by 1% of the time
where the time goes in v6:
time: 26.9 us; the launch traced here: 26.8 us
  Pallas kernels  26 us (97%)
  local copies, waits for them, and re-layouts  0.71 us (3%)
    pallas_call x1, Pallas kernels, per_device(): pl.pallas_call(kernel, out_shape=pltpu.VMEM((1, BLOCK, 1024), BF16), in_s...  26 us
    unnamed x1, local copies, waits for them, and re-layouts  0.71 us

profile of v6, /device:TPU:1, one launch (start us, length us, event | category | flops | bytes accessed | tf_op | source)
XLA Modules:
  0.0 26.8 jit_solution(2055277598180675)
XLA Ops:
  0.0 26.0 %shard_map.46 = bf16[1,128,1024]{2,1,0:T(8,128)(2,1)S(1)} custom-call(bf16[1,512,256]{2,1,0:T(8,128)(2,1)} %q_hbm.1, bf16[1,512,256]{2,1,0:T(8,128)(2,1)} %k_hbm.1, bf16[1,512,256]{2,1,0:T(8,128)(2,1)} %v_hbm.1, bf16[1024,1024]{1,0:T(8,128)(2,1)} %w_hbm.1), custom_call_target="tpu_custom_call" | custom-call | tf_op jit(solution)/shard_map/pallas_call | solution.py:640
  26.1 0.7 %copy.6 = bf16[1,128,1024]{2,1,0:T(8,128)(2,1)} copy(bf16[1,128,1024]{2,1,0:T(8,128)(2,1)S(1)} %shard_map.46) | data formatting | bytes 524288

commit v7 on v6

--- a/solution.py
+++ b/solution.py
@@ -86,9 +86,6 @@
         pltpu.make_async_copy(q_hbm.at[0], q_s, in_sem.at[2]),
         pltpu.make_async_copy(w_hbm, w_s, in_sem.at[3]),
     ]
-    for load in loads:
-        load.start()
-
     barrier = pltpu.get_barrier_semaphore()
 
     def signal(semaphore, seq, head):
@@ -98,7 +95,7 @@
 
     @pl.when(early)
     def _():
-        for other in range(4, 8):
+        for other in (7, 6, 5, 4):
             for j in range(4):
                 signal(barrier, column(other) + j, g)
 
@@ -122,6 +119,9 @@
     @pl.when(zl > 0)
     def _():
         signal(barrier, s - 8, g)
+
+    for load in loads:
+        load.start()
 
     low32 = iota((32, 128), 1) < HD
 

time: 26.9 us -> 26.9 us (level)
  no operation moved by 1% of the time
where the time goes in v7:
time: 26.9 us; the launch traced here: 26.8 us
  Pallas kernels  26 us (97%)
  local copies, waits for them, and re-layouts  0.71 us (3%)
    pallas_call x1, Pallas kernels, per_device(): pl.pallas_call(kernel, out_shape=pltpu.VMEM((1, BLOCK, 1024), BF16), in_s...  26 us
    unnamed x1, local copies, waits for them, and re-layouts  0.71 us

profile of v7, /device:TPU:1, one launch (start us, length us, event | category | flops | bytes accessed | tf_op | source)
XLA Modules:
  0.0 26.8 jit_solution(16544649537193136282)
XLA Ops:
  0.0 26.0 %shard_map.46 = bf16[1,128,1024]{2,1,0:T(8,128)(2,1)S(1)} custom-call(bf16[1,512,256]{2,1,0:T(8,128)(2,1)} %q_hbm.1, bf16[1,512,256]{2,1,0:T(8,128)(2,1)} %k_hbm.1, bf16[1,512,256]{2,1,0:T(8,128)(2,1)} %v_hbm.1, bf16[1024,1024]{1,0:T(8,128)(2,1)} %w_hbm.1), custom_call_target="tpu_custom_call" | custom-call | tf_op jit(solution)/shard_map/pallas_call | solution.py:640
  26.1 0.7 %copy.6 = bf16[1,128,1024]{2,1,0:T(8,128)(2,1)} copy(bf16[1,128,1024]{2,1,0:T(8,128)(2,1)S(1)} %shard_map.46) | data formatting | bytes 524288

commit v8 on v6

--- a/solution.py
+++ b/solution.py
@@ -86,7 +86,7 @@
         pltpu.make_async_copy(q_hbm.at[0], q_s, in_sem.at[2]),
         pltpu.make_async_copy(w_hbm, w_s, in_sem.at[3]),
     ]
-    for load in loads:
+    for load in loads[:3]:
         load.start()
 
     barrier = pltpu.get_barrier_semaphore()
@@ -325,6 +325,7 @@
         for copy in to_right:
             copy.start()
 
+    loads[3].start()
     near_block(1)
     near_block(2)
     pooled_q = dot(pooler(1), q_s[...]) * 0.5**0.5

time: 26.9 us -> 26.9 us (level)
  no operation moved by 1% of the time
where the time goes in v8:
time: 26.9 us; the launch traced here: 26.8 us
  Pallas kernels  26 us (97%)
  local copies, waits for them, and re-layouts  0.71 us (3%)
    pallas_call x1, Pallas kernels, per_device(): pl.pallas_call(kernel, out_shape=pltpu.VMEM((1, BLOCK, 1024), BF16), in_s...  26 us
    unnamed x1, local copies, waits for them, and re-layouts  0.71 us

profile of v8, /device:TPU:1, one launch (start us, length us, event | category | flops | bytes accessed | tf_op | source)
XLA Modules:
  0.0 26.8 jit_solution(2775684152522244180)
XLA Ops:
  0.0 26.0 %shard_map.46 = bf16[1,128,1024]{2,1,0:T(8,128)(2,1)S(1)} custom-call(bf16[1,512,256]{2,1,0:T(8,128)(2,1)} %q_hbm.1, bf16[1,512,256]{2,1,0:T(8,128)(2,1)} %k_hbm.1, bf16[1,512,256]{2,1,0:T(8,128)(2,1)} %v_hbm.1, bf16[1024,1024]{1,0:T(8,128)(2,1)} %w_hbm.1), custom_call_target="tpu_custom_call" | custom-call | tf_op jit(solution)/shard_map/pallas_call | solution.py:641
  26.1 0.7 %copy.6 = bf16[1,128,1024]{2,1,0:T(8,128)(2,1)} copy(bf16[1,128,1024]{2,1,0:T(8,128)(2,1)S(1)} %shard_map.46) | data formatting | bytes 524288
